TPU v7x, 32 devices: a whole 2x2x4 slice. The times are simulated.
32 devices in a mesh: rows: 8 (over z, x), hid: 4 (over y, core).
Axes of the slice: x: 2, y: 2, z: 4, core: 2. Of those that a mesh axis runs over, the one named last changes fastest.
Arguments:
- char_ids: int32 [512, 8], P('rows'), may hold values from 0 to 274
- lang_ids: int32 [512], P('rows'), may hold values from 0 to 7, as said below
- vocab_masks: int32 [8, 275], replicated, may hold values from 0 to 1, as said below
- targets: int32 [2, 512, 8], P(None, 'rows'), may hold values from 0 to 274, as said below
- embedding: bfloat16 [2, 275, 100], replicated, may hold values from -6 to 6
- w_in: bfloat16 [2, 100, 4, 2048], P(None, None, None, 'hid'), may hold values from -0.625 to 0.625
- w_rec: bfloat16 [2, 2048, 4, 2048], P(None, 'rows', None, 'hid'), may hold values from -0.5 to 0.5
- b_in: bfloat16 [2, 4, 2048], P(None, None, 'hid'), may hold values from -3 to 3
- b_rec: bfloat16 [2, 4, 2048], P(None, None, 'hid'), may hold values from -3 to 3
- w_dec: bfloat16 [2, 2048, 275], P(None, 'hid'), may hold values from -0.5 to 0.5
- b_dec: bfloat16 [2, 275], replicated, may hold values from -6 to 6
Outputs:
- total_loss: float32 [], replicated
- grad_embedding: float32 [2, 275, 100], replicated
- grad_w_in: float32 [2, 100, 4, 2048], P(None, None, None, 'hid')
- grad_w_rec: float32 [2, 2048, 4, 2048], P(None, 'rows', None, 'hid')
- grad_b_in: float32 [2, 4, 2048], P(None, None, 'hid')
- grad_b_rec: float32 [2, 4, 2048], P(None, None, 'hid')
- grad_w_dec: float32 [2, 2048, 275], P(None, 'hid')
- grad_b_dec: float32 [2, 275], replicated
Inputs may be any that keep to these rules, and one draw needn't show every extreme that they name: `lang_ids`: rows stand in order of language, and every language has a row. `vocab_masks`: each language allows exactly 192 characters. `targets`: every target is a character that its row's language allows.
All inputs are finite; a program needn't handle non-finite values.
Results may differ from a plain program's by a relative error of at most 0.014.
Values may be sent and summed in bfloat16 or wider, within the bound.
A program may use at most 192 MiB of HBM per device.

v0:
```python
import jax
import jax.numpy as jnp
from jax import lax
from jax.sharding import PartitionSpec as P

highest = lax.Precision.HIGHEST
masked_value = -1000000000.0


def gate_values(preact, unit_count):
    gate_parts = preact.reshape(preact.shape[:-1] + (4, unit_count))
    in_gate = jax.nn.sigmoid(gate_parts[..., 0, :])
    forget_gate = jax.nn.sigmoid(gate_parts[..., 1, :])
    cell_gate = jnp.tanh(gate_parts[..., 2, :])
    out_gate = jax.nn.sigmoid(gate_parts[..., 3, :])
    return (in_gate, forget_gate, cell_gate, out_gate)


def local(
    char_ids, lang_ids, vocab_masks, targets, embedding, w_in, w_rec, b_in, b_rec, w_dec, b_dec
):
    row_devices = lax.axis_size("rows")
    row_count, seq_len = char_ids.shape
    unit_count = w_in.shape[3]
    embed_width = w_in.shape[1]
    vocab_size = embedding.shape[1]
    lang_count = vocab_masks.shape[0]
    loss_scale = 1.0 / (row_count * row_devices * seq_len)
    rec_full = lax.all_gather(w_rec, "rows", axis=1, tiled=True)
    hidden_width = rec_full.shape[1]
    lang_match = lang_ids[:, None] == jnp.arange(lang_count, dtype=jnp.int32)[None, :]
    allowed = jnp.sum(jnp.where(lang_match[:, :, None], vocab_masks[None], 0), axis=1) > 0
    vocab_index = jnp.arange(vocab_size, dtype=jnp.int32)
    groups = [[0], [1]]
    loss_list, embed_list, in_list, rec_list, bias_list, wdec_list, bdec_list = (
        [],
        [],
        [],
        [],
        [],
        [],
        [],
    )
    for group in groups:
        first = group[0]
        count = len(group)
        chars_list, target_list = ([], [])
        for direction in group:
            if direction == 0:
                chars_list.append(char_ids.T)
                target_list.append(targets[0].T)
            else:
                chars_list.append(char_ids[:, ::-1].T)
                target_list.append(targets[1][:, ::-1].T)
        seq_chars = jnp.stack(chars_list, axis=1)
        seq_targets = jnp.stack(target_list, axis=1)
        inputs_seq = jnp.stack([embedding[group[0]][chars_list[0]]], axis=1)
        in_matrix = w_in[first : first + count].reshape(count, embed_width, 4 * unit_count)
        bias_sum = (
            b_in[first : first + count].astype(jnp.float32)
            + b_rec[first : first + count].astype(jnp.float32)
        ).reshape(count, 1, 4 * unit_count)
        gates_in = (
            jnp.einsum("lkbe,kef->lkbf", inputs_seq, in_matrix, preferred_element_type=jnp.float32)
            + bias_sum
        )
        recurrent_matrix = rec_full[first : first + count].reshape(
            count, hidden_width, 4 * unit_count
        )

        def forward_step(state_pair, gate_input):
            complete_state, cell_state = state_pair
            preact = gate_input + jnp.einsum(
                "izd,idl->izl", complete_state, recurrent_matrix, preferred_element_type=jnp.float32
            )
            in_gate, forget_gate, cell_gate, out_gate = gate_values(preact, unit_count)
            cell_next = forget_gate * cell_state + in_gate * cell_gate
            state_low = (out_gate * jnp.tanh(cell_next)).astype(jnp.bfloat16)
            state_next = lax.all_gather(state_low, "hid", axis=2, tiled=True)
            return ((state_next, cell_next), (preact, cell_state, state_low, state_next))

        start_pair = (
            jnp.zeros((count, row_count, hidden_width), jnp.bfloat16),
            jnp.zeros((count, row_count, unit_count), jnp.float32),
        )
        _, (preacts, previous_cells, states_low, states_full) = lax.scan(
            forward_step, start_pair, gates_in
        )
        previous_states = jnp.concatenate(
            [jnp.zeros_like(states_full[:1]), states_full[:-1]], axis=0
        )
        dec_local = w_dec[first : first + count]
        partial_logits = jnp.einsum(
            "lkbu,kuv->lkbv", states_low, dec_local, preferred_element_type=jnp.float32
        )
        logits = lax.psum(partial_logits, "hid")
        logits = logits + b_dec[first : first + count].astype(jnp.float32)[:, None, :]
        masked = jnp.where(allowed[None, None], logits, masked_value)
        log_total = jax.nn.logsumexp(masked, axis=-1)
        target_hot = seq_targets[..., None] == vocab_index
        picked = jnp.sum(jnp.where(target_hot, logits, 0.0), axis=-1)
        loss_list.append(jnp.sum(log_total - picked) * loss_scale)
        probs = jnp.exp(masked - log_total[..., None])
        logit_grad = ((probs - target_hot.astype(jnp.float32)) * loss_scale).astype(jnp.bfloat16)
        bdec_list.append(jnp.sum(logit_grad, axis=(0, 2), dtype=jnp.float32))
        wdec_list.append(
            jnp.einsum("lkbu,lkbv->kuv", states_low, logit_grad, preferred_element_type=jnp.float32)
        )
        dec_back = jnp.einsum(
            "lkbv,kuv->lkbu", logit_grad, dec_local, preferred_element_type=jnp.float32
        )

        def backward_step(grad_pair, saved):
            state_grad, cell_grad = grad_pair
            preact, cell_state, output_gradient = saved
            in_gate, forget_gate, cell_gate, out_gate = gate_values(preact, unit_count)
            cell_next = forget_gate * cell_state + in_gate * cell_gate
            tanh_cell = jnp.tanh(cell_next)
            hidden_grad = output_gradient + state_grad
            out_grad = hidden_grad * tanh_cell
            cell_total = cell_grad + hidden_grad * out_gate * (1.0 - tanh_cell * tanh_cell)
            preact_grad = jnp.stack(
                [
                    cell_total * cell_gate * in_gate * (1.0 - in_gate),
                    cell_total * cell_state * forget_gate * (1.0 - forget_gate),
                    cell_total * in_gate * (1.0 - cell_gate * cell_gate),
                    out_grad * out_gate * (1.0 - out_gate),
                ],
                axis=-2,
            )
            preact_grad = preact_grad.astype(jnp.bfloat16)
            flattened_gradient = preact_grad.reshape(count, row_count, 4 * unit_count)
            partial_terms = jnp.einsum(
                "uil,utl->uit",
                flattened_gradient,
                recurrent_matrix,
                preferred_element_type=jnp.float32,
            )
            state_back = lax.psum_scatter(partial_terms, "hid", scatter_dimension=2, tiled=True)
            return (
                (state_back, cell_total * forget_gate),
                preact_grad.reshape(count, row_count, 4 * unit_count),
            )

        zero_pair = (
            jnp.zeros((count, row_count, unit_count), jnp.float32),
            jnp.zeros((count, row_count, unit_count), jnp.float32),
        )
        _, preactivation_gradients = lax.scan(
            backward_step, zero_pair, (preacts, previous_cells, dec_back), reverse=True
        )
        rec_list.append(
            jnp.einsum(
                "oaid,oaig->adg",
                previous_states,
                preactivation_gradients,
                preferred_element_type=jnp.float32,
            )
        )
        in_list.append(
            jnp.einsum(
                "lkbe,lkbf->kef",
                inputs_seq,
                preactivation_gradients,
                preferred_element_type=jnp.float32,
            )
        )
        bias_list.append(jnp.sum(preactivation_gradients, axis=(0, 2), dtype=jnp.float32))
        input_grad = jnp.einsum(
            "lkbf,kef->lkbe", preactivation_gradients, in_matrix, preferred_element_type=jnp.float32
        )
        char_hot = (seq_chars[..., None] == vocab_index).astype(jnp.float32)
        embed_list.append(jnp.einsum("lkbv,lkbe->kve", char_hot, input_grad, precision=highest))
    rec_terms = jnp.concatenate(rec_list, axis=0).reshape(2, hidden_width, 4, unit_count)
    grad_w_rec = lax.psum_scatter(rec_terms, "rows", scatter_dimension=1, tiled=True)
    loss_sum = loss_list[0]
    for extra in loss_list[1:]:
        loss_sum = loss_sum + extra
    grad_w_in, grad_bias, grad_w_dec, grad_b_dec, total_loss = lax.psum(
        (
            jnp.concatenate(in_list, axis=0).reshape(2, embed_width, 4, unit_count),
            jnp.concatenate(bias_list, axis=0).reshape(2, 4, unit_count),
            jnp.concatenate(wdec_list, axis=0),
            jnp.concatenate(bdec_list, axis=0),
            loss_sum,
        ),
        "rows",
    )
    grad_embedding = lax.psum(jnp.concatenate(embed_list, axis=0), ("rows", "hid"))
    return (
        total_loss,
        grad_embedding,
        grad_w_in,
        grad_w_rec,
        grad_bias,
        grad_bias,
        grad_w_dec,
        grad_b_dec,
    )


def solution(mesh):
    placed = (
        P("rows", None),
        P("rows"),
        P(),
        P(None, "rows", None),
        P(),
        P(None, None, None, "hid"),
        P(None, "rows", None, "hid"),
        P(None, None, "hid"),
        P(None, None, "hid"),
        P(None, "hid", None),
        P(),
    )
    return jax.shard_map(
        local,
        mesh=mesh,
        in_specs=placed,
        out_specs=(
            P(),
            P(),
            P(None, None, None, "hid"),
            P(None, "rows", None, "hid"),
            P(None, None, "hid"),
            P(None, None, "hid"),
            P(None, "hid", None),
            P(),
        ),
        check_vma=False,
    )
```

profile of v0, /device:TPU:0, one launch (start us, length us, event | category | flops | bytes accessed | tf_op | source)
XLA Modules:
  0.0 2032.1 jit_solution(6088013207590304557)
XLA Ops:
  19.9 220.7 %all-gather.2.cloned.1.call-done = bf16[2,2048,4,512]{3,2,1,0:T(4,128)(2,1)} async-done(((bf16[2,256,4,512]{3,2,1,0:T(4,128)(2,1)}), bf16[2,2048,4,512]{3,2,1,0:T(4,128)(2,1)}) %all-gather.2.cloned.1.call-update) | async-done | bytes 16777232 | tf_op jit(solution)/shard_map/all_gather | solution.py:29
  240.6 15.7 fusion.164
  256.3 14.4 reshape.1503
  275.2 121.3 %while.81 = (s32[]{:T(128)}, bf16[1,64,2048]{2,0,1:T(2,128)(2,1)S(1)}, f32[1,64,512]{2,0,1:T(1,128)S(1)}, f32[8,1,64,2048]{3,2,1,0:T(8,128)}, f32[8,1,64,512]{3,...) while((s32[]{:T(128)}, ...), condition=%wide.region_9.10_spmd.clone, body=%wide.region_8.9_spmd.clone.sunk | while | flops 537526272 | bytes 15663248 | solution.py:86
  396.5 14.7 reshape.1499
  416.6 136.6 %while.80 = (s32[]{:T(128)}, bf16[1,64,2048]{2,0,1:T(2,128)(2,1)S(1)}, f32[1,64,512]{2,0,1:T(1,128)S(1)}, f32[8,1,64,2048]{3,2,1,0:T(8,128)}, f32[8,1,64,512]{3,...) while((s32[]{:T(128)}, ...), condition=%wide.region_2.3_spmd.clone, body=%wide.region_1.2_spmd.clone.sunk | while | flops 537526272 | bytes 15663248 | solution.py:86
  562.5 38.2 %all-reduce.13.cloned.1.call-done = (f32[8,1,64,275]{3,2,0,1:T(8,128)}, f32[8,1,64,275]{3,2,0,1:T(8,128)}) async-done(((f32[8,1,64,275]{3,2,0,1:T(8,128)}, f32[8,1,64,275]{3,2,0,1:T(8,128)}), (f32[8,1,64,275]{3,2,0,1:T(8,128)}, f32[8,1,64,275]{3,2,0,1:T(8,128)})) %all-reduce.13.cloned.1.call-update) | async-done | bytes 1126416 | tf_op jit(solution)/shard_map/psum | solution.py:96
  613.3 297.8 %while.83 = (s32[]{:T(128)}, f32[1,64,512]{2,1,0:T(8,128)}, f32[1,64,512]{2,1,0:T(8,128)}, bf16[8,1,64,2048]{3,2,1,0:T(8,128)(2,1)S(1)}, f32[8,1,64,512]{3,2,1,0...) while((s32[]{:T(128)}, f32[1,64,512]{2,1,0:T(8,128)}, ...), condition=%wide.region_21.22_spmd.clone, body=%wide.region_19.21_spmd.clone.sunk | while | flops 538607616 | bytes 19136704 | solution.py:149
  629.7 21.0 %reduce-scatter.8.cloned.1.call-done = f32[1,64,512]{2,1,0:T(8,128)} async-done(((f32[1,64,2048]{2,1,0:T(8,128)}), f32[1,64,512]{2,1,0:T(8,128)}) %reduce-scatter.8.cloned.1.call-update) | async-done | bytes 131088 | tf_op jit(solution)/shard_map/while/body/eval_jaxpr/reduce_scatter | solution.py:139
  666.9 21.0 %reduce-scatter.8.cloned.1.call-done = f32[1,64,512]{2,1,0:T(8,128)} async-done(((f32[1,64,2048]{2,1,0:T(8,128)}), f32[1,64,512]{2,1,0:T(8,128)}) %reduce-scatter.8.cloned.1.call-update) | async-done | bytes 131088 | tf_op jit(solution)/shard_map/while/body/eval_jaxpr/reduce_scatter | solution.py:139
  704.1 21.0 %reduce-scatter.8.cloned.1.call-done = f32[1,64,512]{2,1,0:T(8,128)} async-done(((f32[1,64,2048]{2,1,0:T(8,128)}), f32[1,64,512]{2,1,0:T(8,128)}) %reduce-scatter.8.cloned.1.call-update) | async-done | bytes 131088 | tf_op jit(solution)/shard_map/while/body/eval_jaxpr/reduce_scatter | solution.py:139
  741.3 21.0 %reduce-scatter.8.cloned.1.call-done = f32[1,64,512]{2,1,0:T(8,128)} async-done(((f32[1,64,2048]{2,1,0:T(8,128)}), f32[1,64,512]{2,1,0:T(8,128)}) %reduce-scatter.8.cloned.1.call-update) | async-done | bytes 131088 | tf_op jit(solution)/shard_map/while/body/eval_jaxpr/reduce_scatter | solution.py:139
  778.5 21.0 %reduce-scatter.8.cloned.1.call-done = f32[1,64,512]{2,1,0:T(8,128)} async-done(((f32[1,64,2048]{2,1,0:T(8,128)}), f32[1,64,512]{2,1,0:T(8,128)}) %reduce-scatter.8.cloned.1.call-update) | async-done | bytes 131088 | tf_op jit(solution)/shard_map/while/body/eval_jaxpr/reduce_scatter | solution.py:139
  815.8 21.0 %reduce-scatter.8.cloned.1.call-done = f32[1,64,512]{2,1,0:T(8,128)} async-done(((f32[1,64,2048]{2,1,0:T(8,128)}), f32[1,64,512]{2,1,0:T(8,128)}) %reduce-scatter.8.cloned.1.call-update) | async-done | bytes 131088 | tf_op jit(solution)/shard_map/while/body/eval_jaxpr/reduce_scatter | solution.py:139
  853.0 21.0 %reduce-scatter.8.cloned.1.call-done = f32[1,64,512]{2,1,0:T(8,128)} async-done(((f32[1,64,2048]{2,1,0:T(8,128)}), f32[1,64,512]{2,1,0:T(8,128)}) %reduce-scatter.8.cloned.1.call-update) | async-done | bytes 131088 | tf_op jit(solution)/shard_map/while/body/eval_jaxpr/reduce_scatter | solution.py:139
  890.2 21.0 %reduce-scatter.8.cloned.1.call-done = f32[1,64,512]{2,1,0:T(8,128)} async-done(((f32[1,64,2048]{2,1,0:T(8,128)}), f32[1,64,512]{2,1,0:T(8,128)}) %reduce-scatter.8.cloned.1.call-update) | async-done | bytes 131088 | tf_op jit(solution)/shard_map/while/body/eval_jaxpr/reduce_scatter | solution.py:139
  914.8 297.5 %while.82 = (s32[]{:T(128)}, f32[1,64,512]{2,1,0:T(8,128)}, f32[1,64,512]{2,1,0:T(8,128)S(1)}, bf16[8,1,64,2048]{3,2,1,0:T(8,128)(2,1)S(1)}, f32[8,1,64,512]{3,2...) while((s32[]{:T(128)}, f32[1,64,512]{2,1,0:T(8,128)}, ...), condition=%wide.region_18.19_spmd.clone, body=%wide.region_16.18_spmd.clone.sunk | while | flops 538607616 | bytes 19136704 | solution.py:149
  930.8 21.6 %reduce-scatter.6.cloned.1.call-done = f32[1,64,512]{2,1,0:T(8,128)} async-done(((f32[1,64,2048]{2,1,0:T(8,128)}), f32[1,64,512]{2,1,0:T(8,128)}) %reduce-scatter.6.cloned.1.call-update) | async-done | bytes 131088 | tf_op jit(solution)/shard_map/while/body/eval_jaxpr/reduce_scatter | solution.py:139
  967.9 21.6 %reduce-scatter.6.cloned.1.call-done = f32[1,64,512]{2,1,0:T(8,128)} async-done(((f32[1,64,2048]{2,1,0:T(8,128)}), f32[1,64,512]{2,1,0:T(8,128)}) %reduce-scatter.6.cloned.1.call-update) | async-done | bytes 131088 | tf_op jit(solution)/shard_map/while/body/eval_jaxpr/reduce_scatter | solution.py:139
  1005.1 21.6 %reduce-scatter.6.cloned.1.call-done = f32[1,64,512]{2,1,0:T(8,128)} async-done(((f32[1,64,2048]{2,1,0:T(8,128)}), f32[1,64,512]{2,1,0:T(8,128)}) %reduce-scatter.6.cloned.1.call-update) | async-done | bytes 131088 | tf_op jit(solution)/shard_map/while/body/eval_jaxpr/reduce_scatter | solution.py:139
  1042.2 21.6 %reduce-scatter.6.cloned.1.call-done = f32[1,64,512]{2,1,0:T(8,128)} async-done(((f32[1,64,2048]{2,1,0:T(8,128)}), f32[1,64,512]{2,1,0:T(8,128)}) %reduce-scatter.6.cloned.1.call-update) | async-done | bytes 131088 | tf_op jit(solution)/shard_map/while/body/eval_jaxpr/reduce_scatter | solution.py:139
  1079.3 21.6 %reduce-scatter.6.cloned.1.call-done = f32[1,64,512]{2,1,0:T(8,128)} async-done(((f32[1,64,2048]{2,1,0:T(8,128)}), f32[1,64,512]{2,1,0:T(8,128)}) %reduce-scatter.6.cloned.1.call-update) | async-done | bytes 131088 | tf_op jit(solution)/shard_map/while/body/eval_jaxpr/reduce_scatter | solution.py:139
  1116.4 21.6 %reduce-scatter.6.cloned.1.call-done = f32[1,64,512]{2,1,0:T(8,128)} async-done(((f32[1,64,2048]{2,1,0:T(8,128)}), f32[1,64,512]{2,1,0:T(8,128)}) %reduce-scatter.6.cloned.1.call-update) | async-done | bytes 131088 | tf_op jit(solution)/shard_map/while/body/eval_jaxpr/reduce_scatter | solution.py:139
  1153.6 21.6 %reduce-scatter.6.cloned.1.call-done = f32[1,64,512]{2,1,0:T(8,128)} async-done(((f32[1,64,2048]{2,1,0:T(8,128)}), f32[1,64,512]{2,1,0:T(8,128)}) %reduce-scatter.6.cloned.1.call-update) | async-done | bytes 131088 | tf_op jit(solution)/shard_map/while/body/eval_jaxpr/reduce_scatter | solution.py:139
  1190.7 21.6 %reduce-scatter.6.cloned.1.call-done = f32[1,64,512]{2,1,0:T(8,128)} async-done(((f32[1,64,2048]{2,1,0:T(8,128)}), f32[1,64,512]{2,1,0:T(8,128)}) %reduce-scatter.6.cloned.1.call-update) | async-done | bytes 131088 | tf_op jit(solution)/shard_map/while/body/eval_jaxpr/reduce_scatter | solution.py:139
  1219.0 9.8 convolution_bitcast_fusion
  1238.5 18.6 pad_maximum_fusion
  1261.4 37.7 %all-reduce.2 = (f32[]{:T(128)}, f32[2,4,512]{2,1,0:T(4,128)S(1)}, f32[2,275]{1,0:T(2,128)}) all-reduce(f32[]{:T(128)S(6)} %add.602, f32[2,4,512]{2,1,0:T(4,128)S(1)} %pad_maximum_fusion.4, f32[2,275]{1,0:T(2,128)S(1)} %pad_maximum_fusion.5), channel_id=1, replica_groups=mesh['rows'=8,'hid'=4] {'rows'}, use_global_device_ids=true, to_apply=%region_15.16 | all-reduce | flops 4647 | bytes 37176 | tf_op jit(solution)/shard_map/psum | solution.py:179
  1299.2 45.5 %all-reduce.9.cloned.1.call-done = f32[2,275,100]{2,1,0:T(8,128)} async-done(((f32[2,275,100]{2,1,0:T(8,128)}), f32[2,275,100]{2,1,0:T(8,128)}) %all-reduce.9.cloned.1.call-update) | async-done | bytes 220016 | tf_op jit(solution)/shard_map/psum | solution.py:189
  1346.5 125.2 %all-reduce.11.cloned.1.call-done = (f32[2,100,4,512]{3,1,2,0:T(8,128)}, f32[2,512,275]{1,2,0:T(8,128)}) async-done(((f32[2,100,4,512]{3,1,2,0:T(8,128)}, f32[2,512,275]{1,2,0:T(8,128)}), (f32[2,100,4,512]{3,1,2,0:T(8,128)}, f32[2,512,275]{1,2,0:T(8,128)})) %all-reduce.11.cloned.1.call-update) | async-done | bytes 2764816 | tf_op jit(solution)/shard_map/psum | solution.py:179
  1477.3 540.2 %reduce-scatter.4.cloned.1.call-done = f32[2,256,4,512]{3,1,2,0:T(8,128)} async-done(((f32[2,2048,4,512]{3,1,2,0:T(8,128)}), f32[2,256,4,512]{3,1,2,0:T(8,128)}) %reduce-scatter.4.cloned.1.call-update) | async-done | bytes 4194320 | tf_op jit(solution)/shard_map/reduce_scatter | solution.py:175
  2017.6 6.9 copy.151
  (550 shorter events, 575.3 us)
Async XLA Ops:
  7.2 233.3 %all-gather.2.cloned.1.call-start = ((), (), s32[]{:S(2)}) async-start(), calls=%async_computation.3 | async-start | bytes 18874368 | tf_op jit(solution)/shard_map/all_gather | solution.py:29
  8.0 592.8 %all-reduce.13.cloned.1.call-start = ((), (), s32[]{:S(2)}) async-start(), calls=%async_computation.7 | async-start | bytes 3145728 | tf_op jit(solution)/shard_map/psum | solution.py:96
  9.3 7.9 copy-start.10
  9.5 4.9 copy-start.9
  11.2 6.0 copy-start.16
  12.6 4.6 copy-start.18
  396.5 14.7 copy-start.6
  554.2 5.2 copy-start.36
  554.2 5.2 copy-start.29
  600.8 5.1 copy-start.4
  613.3 37.3 %reduce-scatter.8.cloned.1.call-start = ((), (), s32[]{:S(2)}) async-start(), calls=%async_computation.9 | async-start | bytes 655360 | tf_op jit(solution)/shard_map/while/body/eval_jaxpr/reduce_scatter | solution.py:139
  650.6 37.2 %reduce-scatter.8.cloned.1.call-start = ((), (), s32[]{:S(2)}) async-start(), calls=%async_computation.9 | async-start | bytes 655360 | tf_op jit(solution)/shard_map/while/body/eval_jaxpr/reduce_scatter | solution.py:139
  687.9 37.2 %reduce-scatter.8.cloned.1.call-start = ((), (), s32[]{:S(2)}) async-start(), calls=%async_computation.9 | async-start | bytes 655360 | tf_op jit(solution)/shard_map/while/body/eval_jaxpr/reduce_scatter | solution.py:139
  725.1 37.2 %reduce-scatter.8.cloned.1.call-start = ((), (), s32[]{:S(2)}) async-start(), calls=%async_computation.9 | async-start | bytes 655360 | tf_op jit(solution)/shard_map/while/body/eval_jaxpr/reduce_scatter | solution.py:139
  762.3 37.2 %reduce-scatter.8.cloned.1.call-start = ((), (), s32[]{:S(2)}) async-start(), calls=%async_computation.9 | async-start | bytes 655360 | tf_op jit(solution)/shard_map/while/body/eval_jaxpr/reduce_scatter | solution.py:139
  799.5 37.2 %reduce-scatter.8.cloned.1.call-start = ((), (), s32[]{:S(2)}) async-start(), calls=%async_computation.9 | async-start | bytes 655360 | tf_op jit(solution)/shard_map/while/body/eval_jaxpr/reduce_scatter | solution.py:139
  836.7 37.2 %reduce-scatter.8.cloned.1.call-start = ((), (), s32[]{:S(2)}) async-start(), calls=%async_computation.9 | async-start | bytes 655360 | tf_op jit(solution)/shard_map/while/body/eval_jaxpr/reduce_scatter | solution.py:139
  873.9 37.2 %reduce-scatter.8.cloned.1.call-start = ((), (), s32[]{:S(2)}) async-start(), calls=%async_computation.9 | async-start | bytes 655360 | tf_op jit(solution)/shard_map/while/body/eval_jaxpr/reduce_scatter | solution.py:139
  915.2 37.2 %reduce-scatter.6.cloned.1.call-start = ((), (), s32[]{:S(2)}) async-start(), calls=%async_computation.8 | async-start | bytes 655360 | tf_op jit(solution)/shard_map/while/body/eval_jaxpr/reduce_scatter | solution.py:139
  952.4 37.1 %reduce-scatter.6.cloned.1.call-start = ((), (), s32[]{:S(2)}) async-start(), calls=%async_computation.8 | async-start | bytes 655360 | tf_op jit(solution)/shard_map/while/body/eval_jaxpr/reduce_scatter | solution.py:139
  989.5 37.1 %reduce-scatter.6.cloned.1.call-start = ((), (), s32[]{:S(2)}) async-start(), calls=%async_computation.8 | async-start | bytes 655360 | tf_op jit(solution)/shard_map/while/body/eval_jaxpr/reduce_scatter | solution.py:139
  1026.6 37.1 %reduce-scatter.6.cloned.1.call-start = ((), (), s32[]{:S(2)}) async-start(), calls=%async_computation.8 | async-start | bytes 655360 | tf_op jit(solution)/shard_map/while/body/eval_jaxpr/reduce_scatter | solution.py:139
  1063.8 37.1 %reduce-scatter.6.cloned.1.call-start = ((), (), s32[]{:S(2)}) async-start(), calls=%async_computation.8 | async-start | bytes 655360 | tf_op jit(solution)/shard_map/while/body/eval_jaxpr/reduce_scatter | solution.py:139
  1100.9 37.1 %reduce-scatter.6.cloned.1.call-start = ((), (), s32[]{:S(2)}) async-start(), calls=%async_computation.8 | async-start | bytes 655360 | tf_op jit(solution)/shard_map/while/body/eval_jaxpr/reduce_scatter | solution.py:139
  1138.0 37.1 %reduce-scatter.6.cloned.1.call-start = ((), (), s32[]{:S(2)}) async-start(), calls=%async_computation.8 | async-start | bytes 655360 | tf_op jit(solution)/shard_map/while/body/eval_jaxpr/reduce_scatter | solution.py:139
  1175.2 37.1 %reduce-scatter.6.cloned.1.call-start = ((), (), s32[]{:S(2)}) async-start(), calls=%async_computation.8 | async-start | bytes 655360 | tf_op jit(solution)/shard_map/while/body/eval_jaxpr/reduce_scatter | solution.py:139
  1212.3 132.4 %all-reduce.9.cloned.1.call-start = ((), (), s32[]{:S(2)}) async-start(), calls=%async_computation.4 | async-start | bytes 573440 | tf_op jit(solution)/shard_map/psum | solution.py:189
  1212.3 4.4 copy-start.17
  1216.7 255.0 %all-reduce.11.cloned.1.call-start = ((), (), s32[]{:S(2)}) async-start(), calls=%async_computation.6 | async-start | bytes 5701632 | tf_op jit(solution)/shard_map/psum | solution.py:179
  1219.0 9.8 copy-start.19
  1232.1 785.5 %reduce-scatter.4.cloned.1.call-start = ((), (), s32[]{:S(2)}) async-start(), calls=%async_computation.5 | async-start | bytes 37748736 | tf_op jit(solution)/shard_map/reduce_scatter | solution.py:175
  1299.2 725.3 %copy-start.24 = (f32[2,4,512]{2,1,0:T(4,128)}, f32[2,4,512]{2,1,0:T(4,128)S(1)}, u32[]{:S(2)}) copy-start(f32[2,4,512]{2,1,0:T(4,128)S(1)} %get-tuple-element.1337) | copy-start | bytes 49156
  (26 other events, 54.1 us)
Sparse Core Ops, SparseCore 0:
  10.2 230.2 all-gather.1
  559.5 41.2 all-reduce.12
  628.9 21.6 reduce-scatter.7
  666.2 21.6 reduce-scatter.7
  703.4 21.6 reduce-scatter.7
  740.6 21.6 reduce-scatter.7
  777.8 21.6 reduce-scatter.7
  815.0 21.6 reduce-scatter.7
  852.2 21.6 reduce-scatter.7
  889.4 21.6 reduce-scatter.7
  930.7 21.6 reduce-scatter.5
  967.8 21.6 reduce-scatter.5
  1005.0 21.6 reduce-scatter.5
  1042.1 21.6 reduce-scatter.5
  1079.2 21.6 reduce-scatter.5
  1116.3 21.6 reduce-scatter.5
  1153.5 21.6 reduce-scatter.5
  1190.6 21.6 reduce-scatter.5
  1219.1 125.5 all-reduce.8
  1349.2 122.4 all-reduce.10
  1475.5 542.0 reduce-scatter.3
where the time goes:
time: 2040 us; the launch traced here: 2030 us
  waiting for transfers between devices  1310 us (64%)
  matrix products  243 us (12%)
  local copies, waits for them, and re-layouts  182 us (9%)
  other arithmetic  136 us (7%)
  blocking collectives  131 us (6%)
    reduce_scatter x1, waiting for transfers between devices, local(): lax.psum_scatter(rec_terms, 'rows', scatter_dimension=1, tiled=True)  540 us
    reduce_scatter x16, waiting for transfers between devices, backward_step(): lax.psum_scatter(partial_terms, 'hid', scatter_dimension=2, tiled=True)  340 us
    all_gather x1, waiting for transfers between devices, local(): rec_full = lax.all_gather(w_rec, 'rows', axis=1, tiled=True)  221 us
    psum x1, waiting for transfers between devices, local(): lax.psum((jnp.concatenate(in_list, axis=0).reshape(2, embed_width, 4, uni...  125 us
    dot_general x16, matrix products, backward_step(): jnp.einsum('uil,utl->uit', flattened_gradient, recurrent_matrix, preferre...  109 us
    all_gather x16, blocking collectives, forward_step(): state_next = lax.all_gather(state_low, 'hid', axis=2, tiled=True)  93.8 us
    dot_general x16, matrix products, forward_step(): jnp.einsum('izd,idl->izl', complete_state, recurrent_matrix, preferred_el...  92.9 us
    psum x1, waiting for transfers between devices, local(): lax.psum(jnp.concatenate(embed_list, axis=0), ('rows', 'hid'))  45.5 us
  transfers between devices with their start and end apart: 21, of which 21 were waited for; matrix products, arithmetic and copies ran while one was open for 4% of the time, Pallas kernels for 0%

commit v1 on v0

v1 whole, which is shorter than its diff:
```python
import functools
from typing import NamedTuple

import jax
import jax.numpy as jnp
from jax import lax
from jax.experimental import pallas as pl
from jax.experimental.pallas import tpu as pltpu
from jax.sharding import PartitionSpec as P

MESH = pl.DeviceIdType.MESH
F32 = jnp.float32
BF16 = jnp.bfloat16
masked_value = -1000000000.0


def ceil_to(n, m):
    return (n + m - 1) // m * m


class Dims(NamedTuple):
    R: int
    RR: int
    Hy: int
    H: int
    KR: int
    U: int
    RL: int
    L: int
    V: int
    E: int
    LANGS: int
    scale: float

    @property
    def U2(self):
        return 2 * self.U

    @property
    def NR(self):
        return 2 * self.RL

    @property
    def VP(self):
        return ceil_to(self.V, 128)

    @property
    def VB(self):
        return ceil_to(self.V, 16)

    @property
    def EP(self):
        return ceil_to(self.E + 2, 128)

    @property
    def EW(self):
        return ceil_to(self.E + 2, 16)

    @property
    def V8(self):
        return ceil_to(self.V, 8)

    @property
    def VS(self):
        return self.V8 + 8

    @property
    def peers(self):
        far = [(1, k) for k in range(1, self.Hy)]
        beside = [(0, k) for k in range(1, self.Hy)]
        return far + beside + [(1, 0)]


Z_STEPS = ((1, 0), (1, 1), (0, 1))


def dot(a, b):
    return jnp.dot(a, b, preferred_element_type=F32)


def dot_nt(a, b):
    return lax.dot_general(a, b, (((1,), (1,)), ((), ())), preferred_element_type=F32)


def dot_tn(a, b):
    return lax.dot_general(a, b, (((0,), (0,)), ((), ())), preferred_element_type=F32)


def flip(bit, step):
    return 1 - bit if step else bit


def kernel(
    dims,
    ids_in, win_in, wrec_in, wdec_in, emb_ref, bdec_ref, mask_ref,
    grec_out, gwin_out, gwd_out, small_out,
    ids, win, W, wd, x, xp, allowed, acc, st, stp, gs, cell, lg, lgp, lossv, gb,
    dh, cg, pg, pgx, psend, precv, dW, gwin, gemb, gwd, gwd_s, gwd_r, gwin_s, gwin_r, recvB, esend, erecv,
    lsem, ids_s, ids_r, win_s2, win_r2, wdy_s, wdy_r, wdc_s, wdc_r, wz_s, wz_r, wx_s, wx_r, wc_s, wc_r, xp_s, xp_r,
    f_s, f_r, stp_s, stp_r, lgp_s, lgp_r, b_s, b_r, pgx_s, pgx_r,
    gwdr_s, gwdr_r, gwdz_s, gwdz_r, gwr_s, gwr_r, gwz_s, gwz_r, B_s, B_r, C_s, C_r, e_s, e_r,
):
    R, RR, Hy, U, U2, NR, L, VP = dims.R, dims.RR, dims.Hy, dims.U, dims.U2, dims.NR, dims.L, dims.VP
    KR, EW, VB, V8, VS = dims.KR, dims.EW, dims.VB, dims.V8, dims.VS
    peers = dims.peers
    rho, hid = lax.axis_index("rows"), lax.axis_index("hid")
    d, g, r = rho // (R // 2), lax.rem(rho // RR, 2), lax.rem(rho, RR)
    y, c = hid // 2, lax.rem(hid, 2)
    mine = y * 2 + g
    part = d * 2 + g

    def dev(dd, gg, rr, yy, cc):
        return (dd * (R // 2) + gg * RR + rr, yy * 2 + cc)

    def copy_to(src, dst, send, recv, device):
        return pltpu.make_async_remote_copy(
            src_ref=src, dst_ref=dst, send_sem=send, recv_sem=recv, device_id=device, device_id_type=MESH
        )

    def add_r(step):
        return lax.rem(r + step, RR)

    def add_y(step):
        return lax.rem(y + step, Hy)

    def rows_of(dd, gg, rr):
        index = dd * (R // 2) + gg * RR + rr
        per = U // KR
        block = index // per
        hid_of, g_of = block // 2, lax.rem(block, 2)
        chip = (hid_of // 2) * 2 + g_of
        row = chip * U2 + lax.rem(hid_of, 2) * U + lax.rem(index, per) * KR
        return pl.ds(pl.multiple_of(row, KR), KR)

    def chip_rows(m):
        return pl.ds(pl.multiple_of(m * U2, U2), U2)

    partner = dev(d, g, r, y, 1 - c)

    def z_dev(j):
        return dev(flip(d, Z_STEPS[j][0]), flip(g, Z_STEPS[j][1]), r, y, c)

    def r_dev(step):
        return dev(d, g, add_r(step), y, c)

    def y_dev(step):
        return dev(d, g, r, add_y(step), c)

    def peer_dev(p):
        return dev(d, flip(g, peers[p][0]), r, add_y(peers[p][1]), c)

    barrier = pltpu.get_barrier_semaphore()
    greeted = [z_dev(j) for j in range(3)] + [r_dev(k) for k in range(1, RR)] + [partner]
    greeted += [peer_dev(p) for p in range(len(peers)) if peers[p] != (1, 0)]
    for device in greeted:
        pl.semaphore_signal(barrier, inc=1, device_id=device, device_id_type=MESH)
    pl.semaphore_wait(barrier, len(greeted))

    def ids_copy(j):
        return copy_to(ids_in.at[flip(d, Z_STEPS[j][0]), c], ids.at[part], ids_s.at[j], ids_r.at[j], z_dev(j))

    def wz_copy(j):
        there = wrec_in.at[flip(d, Z_STEPS[j][0]), flip(g, Z_STEPS[j][1])]
        return copy_to(there, W.at[c, :, rows_of(d, g, r), :], wz_s.at[j], wz_r.at[j], z_dev(j))

    def z_block(j):
        steps = Z_STEPS[j] if j < 3 else (0, 0)
        return flip(d, steps[0]), flip(g, steps[1])

    def w_block(j, k):
        dd, gg = z_block(j)
        return W.at[c, :, rows_of(dd, gg, lax.rem(r + RR - k, RR)), :]

    def wx_copy(j, k):
        return copy_to(w_block(j, 0), w_block(j, 0), wx_s.at[j, k - 1], wx_r.at[j, k - 1], r_dev(k))

    def wc_copy(j, k):
        return copy_to(w_block(j, k), w_block(j, k), wc_s.at[j, k], wc_r.at[j, k], partner)

    def wd_rows(yy):
        return wd.at[pl.ds(yy * 2, 2), c]

    def wdy_copy(k):
        return copy_to(wdec_in.at[d], wd_rows(y), wdy_s.at[k - 1], wdy_r.at[k - 1], y_dev(k))

    def wdc_copy(k):
        yy = lax.rem(y + Hy - k, Hy)
        return copy_to(wd_rows(yy), wd_rows(yy), wdc_s.at[k], wdc_r.at[k], partner)

    win_copy = copy_to(win_in.at[d, g], win.at[c], win_s2.at[0], win_r2.at[0], partner)
    own_ids = pltpu.make_async_copy(ids_in.at[d, c], ids.at[part], lsem.at[0])
    own_win = pltpu.make_async_copy(win_in.at[d, g], win.at[c], lsem.at[1])
    own_wd = pltpu.make_async_copy(wdec_in.at[d], wd_rows(y), lsem.at[2])
    own_w = pltpu.make_async_copy(wrec_in.at[d, g], w_block(3, 0), lsem.at[3])

    own_ids.start()
    own_win.start()
    own_w.start()
    own_wd.start()
    for j in range(3):
        ids_copy(j).start()
    win_copy.start()
    for j in range(3):
        wz_copy(j).start()
    for k in range(1, Hy):
        wdy_copy(k).start()

    dW[...] = jnp.zeros_like(dW)
    gwin[...] = jnp.zeros_like(gwin)
    gemb[...] = jnp.zeros_like(gemb)
    lossv[...] = jnp.zeros_like(lossv)
    gb[...] = jnp.zeros_like(gb)
    cg[...] = jnp.zeros_like(cg)
    cell[0] = jnp.zeros_like(cell[0])

    own_w.wait()
    for k in range(1, RR):
        wx_copy(3, k).start()
    wc_copy(3, 0).start()

    own_ids.wait()
    for j in range(3):
        ids_copy(j).wait_recv()

    lane = lax.broadcasted_iota(jnp.int32, (NR, 128), 1)
    vocab = lax.broadcasted_iota(jnp.int32, (NR, VP), 1).astype(F32)

    def id_column(at):
        held = ids[...].reshape(NR, 128)
        return jnp.sum(jnp.where(lane == at, held, 0.0), axis=1, keepdims=True)

    def char_hot(t):
        return jnp.where(vocab == id_column(t), 1.0, 0.0).astype(BF16)

    lang_lane = lax.broadcasted_iota(jnp.int32, (NR, mask_ref.shape[0]), 1).astype(F32)
    lang_hot = jnp.where(lang_lane == id_column(2 * L), 1.0, 0.0).astype(BF16)
    allowed[...] = dot(lang_hot, mask_ref[...])

    @pl.loop(0, L)
    def _(t):
        x[t] = dot(char_hot(t), emb_ref[d]).astype(BF16)

    xp_copy = copy_to(x, xp, xp_s.at[0], xp_r.at[0], partner)
    xp_copy.start()

    own_wd.wait()
    wdc_copy(0).start()
    own_win.wait()
    win_copy.wait_recv()

    def f_copy(t, p):
        slot = lax.rem(t, 2)
        return copy_to(st.at[t, mine], st.at[t, mine], f_s.at[slot, p], f_r.at[slot, p], peer_dev(p))

    def gates(t):
        for cc in range(2):
            si = jax.nn.sigmoid(acc[cc, 0])
            sf = jax.nn.sigmoid(acc[cc, 1])
            tg = jnp.tanh(acc[cc, 2])
            so = jax.nn.sigmoid(acc[cc, 3])
            new = sf * cell[t, cc] + si * tg
            cell[t + 1, cc] = new
            st[t, mine, :, cc * U : (cc + 1) * U] = (so * jnp.tanh(new)).astype(BF16)
            gs[t, 0, cc] = si
            gs[t, 1, cc] = sf
            gs[t, 2, cc] = tg
            gs[t, 3, cc] = so

    def peer_block(p):
        yy = lax.rem(y + Hy - peers[p][1], Hy)
        return yy * 2 + flip(g, peers[p][0])

    for cc in range(2):
        for q in range(4):
            acc[cc, q] = dot(x[0], win[cc, q])
    gates(0)
    for p in range(len(peers)):
        f_copy(0, p).start()

    order = (2, 0, 1)
    for k in range(1, Hy):
        wdy_copy(k).wait_recv()
        wdc_copy(k).start()
    done = [3]
    for j in order:
        wz_copy(j).wait_recv()
        for k in range(1, RR):
            wx_copy(j, k).start()
        wc_copy(j, 0).start()
        last = done[-1]
        for k in range(1, RR):
            wx_copy(last, k).wait_recv()
            wc_copy(last, k).start()
        done.append(j)
    for k in range(1, RR):
        wx_copy(done[-1], k).wait_recv()
        wc_copy(done[-1], k).start()
    for j in range(4):
        for k in range(RR):
            other = W.at[1 - c, :, rows_of(*z_block(j), lax.rem(r + RR - k, RR)), :]
            copy_to(other, other, wc_s.at[j, k], wc_r.at[j, k], partner).wait_recv()
    for k in range(Hy):
        yy = lax.rem(y + Hy - k, Hy)
        other = wd.at[pl.ds(yy * 2, 2), 1 - c]
        copy_to(other, other, wdc_s.at[k], wdc_r.at[k], partner).wait_recv()

    def stp_copy(t):
        return copy_to(st.at[t], stp.at[t], stp_s.at[t], stp_r.at[t], partner)

    def lgp_copy(t):
        return copy_to(lg.at[t], lgp.at[t], lgp_s.at[t], lgp_r.at[t], partner)

    def decode(t):
        stp_copy(t).start()
        logits = bdec_ref[d]
        for m in range(2 * Hy):
            logits = logits + dot(st[t, m], wd[m].reshape(U2, VP))
        masked = jnp.where(allowed[...] > 0.5, logits, masked_value)
        top = jnp.max(masked, axis=1, keepdims=True)
        powers = jnp.exp(masked - top)
        total = jnp.sum(powers, axis=1, keepdims=True)
        hot = vocab == id_column(L + t)
        picked = jnp.sum(jnp.where(hot, logits, 0.0), axis=1, keepdims=True)
        lossv[...] += jnp.broadcast_to(top + jnp.log(total) - picked, (NR, 128))
        grad = ((powers / total - jnp.where(hot, 1.0, 0.0)) * dims.scale).astype(BF16)
        lg[t] = grad
        gb[0:1, :] += jnp.sum(grad.astype(F32), axis=0, keepdims=True)
        lgp_copy(t).start()

    @pl.loop(1, L)
    def _(t):
        before = st.at[t - 1]
        for cc in range(2):
            for q in range(4):
                acc[cc, q] = dot(x[t], win[cc, q]) + dot(before[mine], W[cc, q, chip_rows(mine), :])
        for p in reversed(range(len(peers))):
            f_copy(t - 1, p).wait_recv()
            m = peer_block(p)
            for cc in range(2):
                for q in range(4):
                    acc[cc, q] += dot(before[m], W[cc, q, chip_rows(m), :])
        gates(t)
        for p in range(len(peers)):
            f_copy(t - 1, p).wait_send()
        for p in range(len(peers)):
            f_copy(t, p).start()
        decode(t - 1)

    for j in range(3):
        wz_copy(j).wait_send()
    for j in range(4):
        for k in range(1, RR):
            wx_copy(j, k).wait_send()
        for k in range(RR):
            wc_copy(j, k).wait_send()

    @pl.loop(0, dims.H // U)
    def _(k):
        rows = pl.ds(pl.multiple_of(k * U, U), U)
        for cc in range(2):
            for q in range(4):
                W[cc, q, rows, :] = W[cc, q, rows, :].T

    for p in reversed(range(len(peers))):
        f_copy(L - 1, p).wait_recv()
    decode(L - 1)

    def dec_back(t, cc):
        return dot_nt(lg[t], wd[mine, cc])

    def b_copy(t, p):
        slot = lax.rem(t, 2)
        return copy_to(psend.at[slot, p], precv.at[slot, p], b_s.at[slot, p], b_r.at[slot, p], peer_dev(p))

    def pgx_copy(t):
        slot = lax.rem(t, 2)
        return copy_to(pg.at[slot, 1 - c], pgx.at[slot], pgx_s.at[slot], pgx_r.at[slot], partner)

    def preact_grads(t):
        slot = lax.rem(t, 2)
        for cc in range(2):
            h = dh[cc]
            si, sf, tg, so = gs[t, 0, cc], gs[t, 1, cc], gs[t, 2, cc], gs[t, 3, cc]
            tc = jnp.tanh(cell[t + 1, cc])
            total = cg[cc] + h * so * (1.0 - tc * tc)
            pg[slot, cc, 0] = (total * tg * si * (1.0 - si)).astype(BF16)
            pg[slot, cc, 1] = (total * cell[t, cc] * sf * (1.0 - sf)).astype(BF16)
            pg[slot, cc, 2] = (total * si * (1.0 - tg * tg)).astype(BF16)
            pg[slot, cc, 3] = (h * tc * so * (1.0 - so)).astype(BF16)
            cg[cc] = total * sf
        pgx_copy(t).start()

    def partial(t, m, cc):
        slot = lax.rem(t, 2)
        rows = pl.ds(pl.multiple_of(m * U2 + cc * U, U), U)
        total = None
        for kk in range(2):
            for q in range(4):
                term = dot(pg[slot, kk, q], W[kk, q, rows, :])
                total = term if total is None else total + term
        return total

    def take_state_grad(t):
        slot = lax.rem(t, 2)
        for p in reversed(range(len(peers))):
            b_copy(t, p).wait_recv()
            for cc in range(2):
                dh[cc] += precv[slot, p, :, cc * U : (cc + 1) * U].astype(F32)

    def weight_grads(t, with_rec):
        slot = lax.rem(t, 2)
        pgx_copy(t).wait_recv()
        for q in range(4):
            both = jnp.concatenate([pg[slot, c, q], pgx[slot, q]], axis=0)
            gwin[q] += dot_tn(jnp.concatenate([x[t], xp[t]], axis=0), both)
            if with_rec:
                for m in range(2 * Hy):
                    states = jnp.concatenate([st[t - 1, m], stp[t - 1, m]], axis=0)
                    dW[q, m * U2 : (m + 1) * U2, :] += dot_tn(states, both)
        back = None
        for cc in range(2):
            for q in range(4):
                term = dot_nt(pg[slot, cc, q], win[cc, q])
                back = term if back is None else back + term
        high = back.astype(BF16)
        rest = (back - high.astype(F32)).astype(BF16)
        hot = char_hot(t)
        gemb[...] += dot_tn(hot, high) + dot_tn(hot, rest)

    def gwdr_copy(k):
        return copy_to(gwd_s.at[0], gwd_r.at[k - 1], gwdr_s.at[k - 1], gwdr_r.at[k - 1], r_dev(k))

    def gwdz_copy(j):
        return copy_to(gwd_s.at[1], gwd_out.at[part], gwdz_s.at[j], gwdz_r.at[j], z_dev(j))

    own_gwd = pltpu.make_async_copy(gwd_s.at[1], gwd_out.at[part], lsem.at[0])

    def decoder_grad():
        gwd[...] = jnp.zeros_like(gwd)

        @pl.loop(0, L)
        def _(t):
            columns = pl.ds(pl.multiple_of(c * U, U), U)
            states = jnp.concatenate([st[t, mine, :, columns], stp[t, mine, :, columns]], axis=0)
            gwd[...] += dot_tn(jnp.concatenate([lg[t], lgp[t]], axis=0), states)

        gwd_s[0] = gwd[0:VB].astype(BF16)
        for k in range(1, RR):
            gwdr_copy(k).start()

    def decoder_grad_sum():
        total = gwd[0:VB]
        for k in range(1, RR):
            gwdr_copy(k).wait_recv()
            total = total + gwd_r[k - 1].astype(F32)
        gwd_s[1] = total.astype(BF16)
        for j in range(3):
            gwdz_copy(j).start()
        own_gwd.start()

    for cc in range(2):
        dh[cc] = dec_back(L - 1, cc)

    @pl.loop(0, L)
    def _(t):
        stp_copy(t).wait()
        lgp_copy(t).wait()

    xp_copy.wait()

    @pl.loop(0, L - 1)
    def _(i):
        t = L - 1 - i

        @pl.when(i > 0)
        def _():
            take_state_grad(t + 1)

        @pl.when(i > 1)
        def _():
            pgx_copy(t + 2).wait_send()
            for p in range(len(peers)):
                b_copy(t + 2, p).wait_send()

        preact_grads(t)
        slot = lax.rem(t, 2)
        for p in range(len(peers)):
            m = add_y(peers[p][1]) * 2 + flip(g, peers[p][0])
            for cc in range(2):
                psend[slot, p, :, cc * U : (cc + 1) * U] = partial(t, m, cc).astype(BF16)
            b_copy(t, p).start()
        for cc in range(2):
            dh[cc] = partial(t, mine, cc) + dec_back(t - 1, cc)
        weight_grads(t, True)

        @pl.when(i == 1)
        def _():
            decoder_grad()

        @pl.when(i == 3)
        def _():
            decoder_grad_sum()

    out_steps = ((1, 0), (1, 1), (0, 1), (0, 0))

    def out_rows(i, step):
        dd, gg = flip(d, out_steps[i][0]), flip(g, out_steps[i][1])
        return rows_of(dd, gg, add_r(step))

    def b_out(i, k):
        return copy_to(W.at[0, :, out_rows(i, k), :], recvB.at[k - 1, i], B_s.at[k - 1, i], B_r.at[k - 1, i], r_dev(k))

    def c_out(i):
        return copy_to(W.at[1, :, out_rows(i, 0), :], grec_out.at[part], C_s.at[i], C_r.at[i], z_dev(i))

    own_out = pltpu.make_async_copy(W.at[1, :, out_rows(3, 0), :], grec_out.at[part], lsem.at[1])

    for i in range(4):
        for k in range(1, RR):
            for q in range(4):
                W[0, q, out_rows(i, k), :] = dW[q, out_rows(i, k), :].astype(BF16)
            b_out(i, k).start()

    take_state_grad(1)
    pgx_copy(2).wait_send()
    preact_grads(0)
    weight_grads(0, False)

    def gwr_copy(k):
        return copy_to(gwin_s.at[0], gwin_r.at[k - 1], gwr_s.at[k - 1], gwr_r.at[k - 1], r_dev(k))

    def gwz_copy(j):
        return copy_to(gwin_s.at[1], gwin_out.at[part], gwz_s.at[j], gwz_r.at[j], z_dev(j))

    own_gwin = pltpu.make_async_copy(gwin_s.at[1], gwin_out.at[part], lsem.at[2])

    gwin_s[0] = gwin[:, 0:EW, :].astype(BF16)
    for k in range(1, RR):
        gwr_copy(k).start()

    once = jnp.where(mine == 0, 1.0, 0.0).astype(F32)
    esend[0, 0:V8] = gemb[0:V8]
    esend[0, V8:VS] = jnp.zeros((8, 128), F32)
    for k in range(VP // 128):
        esend[0, V8 + k : V8 + k + 1] = gb[0:1, k * 128 : (k + 1) * 128] * once
    at = V8 + VP // 128
    esend[0, at : at + 1] = jnp.sum(lossv[...], axis=0, keepdims=True) * (once * dims.scale)

    stages = [[partner], [r_dev(k) for k in range(1, RR)], [y_dev(k) for k in range(1, Hy)], [dev(d, 1 - g, r, y, c)]]
    first = [sum(len(s) for s in stages[:n]) for n in range(len(stages) + 1)]

    def e_copy(n, k):
        at = first[n] + k
        return copy_to(esend.at[n], erecv.at[at], e_s.at[at], e_r.at[at], stages[n][k])

    def e_start(n):
        for k in range(len(stages[n])):
            e_copy(n, k).start()

    def e_take(n):
        total = esend[n]
        for k in range(len(stages[n])):
            e_copy(n, k).wait_recv()
            total = total + erecv[first[n] + k]
        esend[n + 1] = total

    e_last = copy_to(esend.at[4], small_out.at[d], e_s.at[first[4]], e_r.at[first[4]], dev(1 - d, g, r, y, c))
    own_small = pltpu.make_async_copy(esend.at[4], small_out.at[d], lsem.at[3])

    def send_rec(i):
        for k in range(1, RR):
            b_out(i, k).wait_recv()
        for q in range(4):
            total = dW[q, out_rows(i, 0), :]
            for k in range(1, RR):
                total = total + recvB[k - 1, i, q].astype(F32)
            W[1, q, out_rows(i, 0), :] = total.astype(BF16)
        if i < 3:
            c_out(i).start()
        else:
            own_out.start()

    e_start(0)
    send_rec(0)
    e_take(0)
    e_start(1)
    send_rec(1)
    total = gwin[:, 0:EW, :]
    for k in range(1, RR):
        gwr_copy(k).wait_recv()
        total = total + gwin_r[k - 1].astype(F32)
    gwin_s[1] = total.astype(BF16)
    for j in range(3):
        gwz_copy(j).start()
    own_gwin.start()
    e_take(1)
    e_start(2)
    send_rec(2)
    e_take(2)
    e_start(3)
    send_rec(3)
    e_take(3)
    e_last.start()
    own_small.start()

    for j in range(3):
        ids_copy(j).wait_send()
    win_copy.wait_send()
    for k in range(1, Hy):
        wdy_copy(k).wait_send()
    for k in range(Hy):
        wdc_copy(k).wait_send()
    for p in range(len(peers)):
        f_copy(L - 1, p).wait_send()
    for t in (2, 1):
        for p in range(len(peers)):
            b_copy(t, p).wait_send()
    pgx_copy(1).wait_send()
    pgx_copy(0).wait_send()
    for k in range(1, RR):
        gwdr_copy(k).wait_send()
        gwr_copy(k).wait_send()
        for i in range(4):
            b_out(i, k).wait_send()
    for n in range(4):
        for k in range(len(stages[n])):
            e_copy(n, k).wait_send()
    for j in range(3):
        gwdz_copy(j).wait()
        gwz_copy(j).wait()
        c_out(j).wait()
    e_last.wait()
    own_gwd.wait()
    own_gwin.wait()
    own_out.wait()
    own_small.wait()


def call_kernel(dims, ids, win, wrec, wdec, emb, bdec, mask):
    R, RR, Hy, U, U2, NR, L, VP = dims.R, dims.RR, dims.Hy, dims.U, dims.U2, dims.NR, dims.L, dims.VP
    KR, EW, EP, VB, VS, H = dims.KR, dims.EW, dims.EP, dims.VB, dims.VS, dims.H
    chips, peers = 2 * Hy, len(dims.peers)
    vmem, sem = pltpu.VMEM, pltpu.SemaphoreType.DMA
    apart = pl.BlockSpec(memory_space=pl.ANY)
    inside = pl.BlockSpec(memory_space=pltpu.VMEM)
    groups = max(RR - 1, 1)
    along = max(Hy - 1, 1)
    stages = 1 + (RR - 1) + (Hy - 1) + 1
    scratch = [
        vmem((4, dims.RL // 2, 128), F32),
        vmem((2, 4, EP, U), BF16),
        vmem((2, 4, H, U), BF16),
        vmem((chips, 2, U, VP), BF16),
        vmem((L, NR, EP), BF16),
        vmem((L, NR, EP), BF16),
        vmem((NR, VP), F32),
        vmem((2, 4, NR, U), F32),
        vmem((L, chips, NR, U2), BF16),
        vmem((L, chips, NR, U2), BF16),
        vmem((L, 4, 2, NR, U), F32),
        vmem((L + 1, 2, NR, U), F32),
        vmem((L, NR, VP), BF16),
        vmem((L, NR, VP), BF16),
        vmem((NR, 128), F32),
        vmem((8, VP), F32),
        vmem((2, NR, U), F32),
        vmem((2, NR, U), F32),
        vmem((2, 2, 4, NR, U), BF16),
        vmem((2, 4, NR, U), BF16),
        vmem((2, peers, NR, U2), BF16),
        vmem((2, peers, NR, U2), BF16),
        vmem((4, H, U), F32),
        vmem((4, EP, U), F32),
        vmem((VP, EP), F32),
        vmem((VP, U), F32),
        vmem((2, VB, U), BF16),
        vmem((groups, VB, U), BF16),
        vmem((2, 4, EW, U), BF16),
        vmem((groups, 4, EW, U), BF16),
        vmem((groups, 4, 4, KR, U), BF16),
        vmem((5, VS, 128), F32),
        vmem((stages, VS, 128), F32),
        sem((4,)),
        sem((3,)), sem((3,)),
        sem((1,)), sem((1,)),
        sem((along,)), sem((along,)),
        sem((Hy,)), sem((Hy,)),
        sem((3,)), sem((3,)),
        sem((4, groups)), sem((4, groups)),
        sem((4, RR)), sem((4, RR)),
        sem((1,)), sem((1,)),
        sem((2, peers)), sem((2, peers)),
        sem((L,)), sem((L,)),
        sem((L,)), sem((L,)),
        sem((2, peers)), sem((2, peers)),
        sem((2,)), sem((2,)),
        sem((groups,)), sem((groups,)),
        sem((3,)), sem((3,)),
        sem((groups,)), sem((groups,)),
        sem((3,)), sem((3,)),
        sem((groups, 4)), sem((groups, 4)),
        sem((3,)), sem((3,)),
        sem((stages + 1,)), sem((stages + 1,)),
    ]
    rows = NR * L
    flops = 2 * rows * (3 * H * 8 * U + 3 * H * VP)
    return pl.pallas_call(
        functools.partial(kernel, dims),
        out_shape=(
            jax.ShapeDtypeStruct((4, 4, KR, U), BF16),
            jax.ShapeDtypeStruct((4, 4, EW, U), BF16),
            jax.ShapeDtypeStruct((4, VB, U), BF16),
            jax.ShapeDtypeStruct((2, VS, 128), F32),
        ),
        in_specs=[apart, apart, apart, apart, inside, inside, inside],
        out_specs=(apart, apart, apart, apart),
        scratch_shapes=scratch,
        cost_estimate=pl.CostEstimate(flops=flops, bytes_accessed=8 << 20, transcendentals=rows * U2 * 8),
        compiler_params=pltpu.CompilerParams(
            collective_id=0, has_side_effects=True, vmem_limit_bytes=62 << 20
        ),
        name="train_step",
    )(ids, win, wrec, wdec, emb, bdec, mask)


def local(
    char_ids, lang_ids, vocab_masks, targets, embedding, w_in, w_rec, b_in, b_rec, w_dec, b_dec
):
    R, hid = lax.axis_size("rows"), lax.axis_size("hid")
    RL, L = char_ids.shape
    E, units = w_in.shape[1], w_in.shape[3]
    V = embedding.shape[1]
    KR = w_rec.shape[1]
    U = units // 2
    dims = Dims(
        R=R, RR=R // 4, Hy=hid // 2, H=units * hid, KR=KR, U=U, RL=RL, L=L, V=V, E=E,
        LANGS=vocab_masks.shape[0], scale=1.0 / (RL * R * L),
    )
    VP, EP = dims.VP, dims.EP

    lang = lang_ids[:, None]
    first = jnp.concatenate([char_ids, targets[0], lang], axis=1)
    second = jnp.concatenate([char_ids[:, ::-1], targets[1][:, ::-1], lang], axis=1)
    ids = jnp.stack([first, second]).astype(F32)
    ids = jnp.pad(ids, ((0, 0), (0, 0), (0, 128 - ids.shape[2]))).reshape(2, 2, RL // 2, 128)
    win = jnp.concatenate([w_in, b_in[:, None], b_rec[:, None]], axis=1)
    win = jnp.pad(win, ((0, 0), (0, EP - E - 2), (0, 0), (0, 0)))
    win = win.reshape(2, EP, 4, 2, U).transpose(0, 3, 2, 1, 4)
    wrec = w_rec.reshape(2, KR, 4, 2, U).transpose(0, 3, 2, 1, 4)
    wdec = jnp.pad(w_dec, ((0, 0), (0, 0), (0, VP - V))).reshape(2, 2, U, VP)
    emb = jnp.concatenate([embedding, jnp.ones((2, V, 2), BF16)], axis=2)
    emb = jnp.pad(emb, ((0, 0), (0, VP - V), (0, EP - E - 2)))
    bdec = jnp.pad(b_dec.astype(F32), ((0, 0), (0, VP - V)))[:, None, :]
    lang_rows = ceil_to(dims.LANGS, 16)
    mask = jnp.pad(vocab_masks.astype(BF16), ((0, lang_rows - dims.LANGS), (0, VP - V)))

    grec, gwin, gwd, small = call_kernel(dims, ids, win, wrec, wdec, emb, bdec, mask)

    grad_w_rec = grec.reshape(2, 2, 4, KR, U).transpose(0, 3, 2, 1, 4).reshape(2, KR, 4, units).astype(F32)
    gwin = gwin.reshape(2, 2, 4, dims.EW, U)
    grad_w_in = gwin[:, :, :, :E].transpose(0, 3, 2, 1, 4).reshape(2, E, 4, units).astype(F32)
    grad_bias = gwin[:, :, :, E].transpose(0, 2, 1, 3).reshape(2, 4, units).astype(F32)
    gwd = gwd.reshape(2, 2, dims.VB, U)[:, :, :V]
    grad_w_dec = gwd.transpose(0, 1, 3, 2).reshape(2, units, V).astype(F32)
    V8 = dims.V8
    grad_embedding = small[:, :V, :E]
    grad_b_dec = small[:, V8 : V8 + VP // 128].reshape(2, VP)[:, :V]
    total_loss = jnp.sum(small[:, V8 + VP // 128, 0])
    return (
        total_loss,
        grad_embedding,
        grad_w_in,
        grad_w_rec,
        grad_bias,
        grad_bias,
        grad_w_dec,
        grad_b_dec,
    )


def solution(mesh):
    placed = (
        P("rows", None),
        P("rows"),
        P(),
        P(None, "rows", None),
        P(),
        P(None, None, None, "hid"),
        P(None, "rows", None, "hid"),
        P(None, None, "hid"),
        P(None, None, "hid"),
        P(None, "hid", None),
        P(),
    )
    return jax.shard_map(
        local,
        mesh=mesh,
        in_specs=placed,
        out_specs=(
            P(),
            P(),
            P(None, None, None, "hid"),
            P(None, "rows", None, "hid"),
            P(None, None, "hid"),
            P(None, None, "hid"),
            P(None, "hid", None),
            P(),
        ),
        check_vma=False,
    )
```

time: 2040 us -> 337 us (0.17)
  waiting for transfers between devices: 1310 us -> 0 us
  Pallas kernels: 0 us -> 287 us
  matrix products: 243 us -> 0 us
  local copies, waits for them, and re-layouts: 182 us -> 38.3 us
  blocking collectives: 131 us -> 0 us
  other arithmetic: 136 us -> 9.4 us
    reduce_scatter x17 -> x0, waiting for transfers between devices: 881 us -> none  [the longest x1 540 us: local(): lax.psum_scatter(rec_terms, 'rows', scatter_dimension=1, tiled=True)]
    pallas_call x0 -> x1, Pallas kernels: none -> 287 us  [call_kernel(): pl.pallas_call(functools.partial(kernel, dims), out_shape=(jax.ShapeDtype...]
    dot_general x48 -> x0, matrix products: 243 us -> none  [the longest x16 109 us: backward_step(): jnp.einsum('uil,utl->uit', flattened_gradient, recurrent_matrix, preferre...]
    all_gather x1 -> x0, waiting for transfers between devices: 221 us -> none  [local(): rec_full = lax.all_gather(w_rec, 'rows', axis=1, tiled=True)]
    psum x3 -> x0, waiting for transfers between devices: 209 us -> none  [the longest x1 125 us: local(): lax.psum((jnp.concatenate(in_list, axis=0).reshape(2, embed_width, 4, uni...]
    all_gather x16 -> x0, blocking collectives: 93.8 us -> none  [forward_step(): state_next = lax.all_gather(state_low, 'hid', axis=2, tiled=True)]
    mul x16 -> x0, other arithmetic: 39.7 us -> none  [backward_step(): cell_total * forget_gate]
    psum x1 -> x0, blocking collectives: 37.7 us -> none  [local(): lax.psum((jnp.concatenate(in_list, axis=0).reshape(2, embed_width, 4, uni...]
  transfers between devices with their start and end apart: 21 -> 0, of which waited for: 21 -> 0; matrix products, arithmetic and copies ran while one was open for 4% -> 0% of each run, Pallas kernels for 0% -> 0%
where the time goes in v1:
time: 337 us; the launch traced here: 335 us
  Pallas kernels  287 us (85%)
  local copies, waits for them, and re-layouts  38.3 us (11%)
  other arithmetic  9.4 us (3%)
    pallas_call x1, Pallas kernels, call_kernel(): pl.pallas_call(functools.partial(kernel, dims), out_shape=(jax.ShapeDtype...  287 us
    convert_element_type x2, local copies, waits for them, and re-layouts, local(): grec.reshape(2, 2, 4, KR, U).transpose(0, 3, 2, 1, 4)  12.2 us
    unnamed x26, local copies, waits for them, and re-layouts  8.5 us

profile of v1, /device:TPU:0, one launch (start us, length us, event | category | flops | bytes accessed | tf_op | source)
XLA Modules:
  0.0 335.4 jit_solution(10088329996451519824)
XLA Ops:
  0.7 0.7 slice_bitcast_fusion.2
  1.4 0.7 rev.6
  2.1 0.7 fusion.8
  2.9 0.7 pad.26.clone
  3.5 1.9 copy.42
  5.4 0.5 copy.43
  5.9 1.4 copy.44
  7.3 2.4 fusion.4
  9.7 1.3 copy.45
  11.0 3.0 copy.46
  14.0 2.3 copy.47
  16.4 0.7 copy.57
  17.1 1.0 pad.28.clone
  18.1 0.7 fusion.7.emb_ref
  18.9 0.6 pad.31.mask_ref
  19.5 0.6 reshape.61.bdec_ref
  20.1 286.9 %train_step.1 = (bf16[4,4,256,256]{3,2,1,0:T(8,128)(2,1)}, bf16[4,4,112,256]{3,2,1,0:T(8,128)(2,1)}, bf16[4,288,256]{2,1,0:T(8,128)(2,1)}, f32[2,288,128]{2,1,0:T(8,128)}) custom-call(f32[2,2,32,128]{3,2,1,0:T(8,128)} %bitcast.49, bf16[2,2,4,128,256]{4,3,2,1,0:T(8,128)(2,1)} %bitcast.44, bf16[2,2,4,256,256]{4,3,2,1,0:T(8,128)(2,1)} %bitcast.43, ...), custom_call_target="tpu_custom_call" | custom-call | flops 30601641984 | bytes 8388608 | tf_op jit(solution)/shard_map/train_step/pallas_call | solution.py:707
  307.0 1.0 slice.30
  308.0 0.9 copy.54
  308.8 0.9 slice_convert_fusion
  309.7 0.7 slice_bitcast_fusion
  310.4 0.6 copy.60
  311.0 1.3 slice_reduce_fusion
  312.3 1.3 convert_bitcast_fusion.1
  313.6 1.3 copy.50
  314.9 2.8 reshape.62
  317.6 2.0 convert_bitcast_fusion
  319.7 5.2 %copy.51 = f32[2,256,4,2,256]{4,3,2,1,0:T(2,128)} copy(f32[2,256,4,2,256]{4,1,2,3,0:T(8,128)S(1)} %convert_bitcast_fusion) | data formatting | bytes 8388608 | tf_op jit(solution)/shard_map/convert_element_type | solution.py:759
  324.9 7.0 %reshape.63 = f32[2,256,4,512]{3,2,1,0:T(4,128)} reshape(f32[2,256,4,2,256]{4,3,2,1,0:T(2,128)} %copy.51) | data formatting | bytes 8388608 | tf_op jit(solution)/shard_map/convert_element_type | solution.py:759
  332.0 0.6 copy.53
  332.6 2.3 reshape.65
  334.8 0.6 copy.62
  (24 shorter events, 0.3 us)
Async XLA Ops:
  0.6 4.8 %copy-start.5 = (bf16[2,4,512]{2,1,0:T(4,128)(2,1)S(1)}, bf16[2,4,512]{2,1,0:T(4,128)(2,1)}, u32[]{:S(2)}) copy-start(bf16[2,4,512]{2,1,0:T(4,128)(2,1)} %param.18) | copy-start | bytes 24580
  0.6 5.3 %copy-start.6 = (bf16[2,4,512]{2,1,0:T(4,128)(2,1)S(1)}, bf16[2,4,512]{2,1,0:T(4,128)(2,1)}, u32[]{:S(2)}) copy-start(bf16[2,4,512]{2,1,0:T(4,128)(2,1)} %param.19) | copy-start | bytes 24580
  14.0 2.4 copy-start
  16.4 1.7 copy-start.2
  16.4 2.5 copy-start.4
  16.4 3.1 copy-start.7
  309.7 25.1 %copy-start.3 = (f32[2,2,4,1,256]{4,2,3,1,0:T(4,128)}, f32[2,2,4,1,256]{4,2,3,1,0:T(4,128)S(1)}, u32[]{:S(2)}) copy-start(f32[2,2,4,1,256]{4,2,3,1,0:T(4,128)S(1)} %copy.55) | copy-start | bytes 49156
  324.9 7.0 %copy-start.1 = (bf16[4,288,256]{2,1,0:T(8,128)(2,1)S(1)}, bf16[4,288,256]{2,1,0:T(8,128)(2,1)}, u32[]{:S(2)}) copy-start(bf16[4,288,256]{2,1,0:T(8,128)(2,1)} %get-tuple-element.15) | copy-start | bytes 1769476

commit v2 on v1

v2 whole, which is shorter than its diff:
```python
import functools
from typing import NamedTuple

import jax
import jax.numpy as jnp
from jax import lax
from jax.experimental import pallas as pl
from jax.experimental.pallas import tpu as pltpu
from jax.sharding import PartitionSpec as P

MESH = pl.DeviceIdType.MESH
F32 = jnp.float32
BF16 = jnp.bfloat16
masked_value = -1000000000.0
AHEAD = 4
BATCHES = 2


def ceil_to(n, m):
    return (n + m - 1) // m * m


class Dims(NamedTuple):
    R: int
    RR: int
    Hy: int
    H: int
    KR: int
    U: int
    RL: int
    L: int
    V: int
    E: int
    LANGS: int
    scale: float

    @property
    def U2(self):
        return 2 * self.U

    @property
    def NR(self):
        return 2 * self.RL

    @property
    def VP(self):
        return ceil_to(self.V, 128)

    @property
    def RB(self):
        return self.NR // BATCHES

    @property
    def QN(self):
        return 1 if self.RR <= 2 else 4

    @property
    def N_IN(self):
        return ceil_to(4 * self.EW, 16 * self.RR)

    @property
    def N_DEC(self):
        return ceil_to(self.V, 16 * self.RR)

    @property
    def P8(self):
        return ceil_to(self.L, 8)

    @property
    def EP(self):
        return ceil_to(self.E + 2, 128)

    @property
    def EW(self):
        return ceil_to(self.E + 2, 16)

    @property
    def V8(self):
        return ceil_to(self.V, 8)

    @property
    def VS(self):
        return ceil_to(self.V8 + 8, 16)

    @property
    def peers(self):
        far = [(1, k) for k in range(1, self.Hy)]
        beside = [(0, k) for k in range(1, self.Hy)]
        return far + beside + [(1, 0)]


Z_STEPS = ((1, 0), (1, 1), (0, 1))


def dot(a, b):
    return jnp.dot(a, b, preferred_element_type=F32)


def dot_nt(a, b):
    return lax.dot_general(a, b, (((1,), (1,)), ((), ())), preferred_element_type=F32)


def dot_tn(a, b):
    return lax.dot_general(a, b, (((0,), (0,)), ((), ())), preferred_element_type=F32)


def flip(bit, step):
    return 1 - bit if step else bit


def kernel(
    dims,
    chars_ref, targets_ref, lang_ref, bias_ref, win_in, wrec_in, wdec_in, emb_ref, bdec_ref, mask_ref,
    grec_out, gwin_out, gwd_out, small_out,
    idsrc, idsall, idtmp, ids, bias, win, W, wd, x, xp, allowed, acc, st, stp, gs, cell, lg, lgp, lossv, gb,
    dh, cg, pg, pgx, psend, precv, dW, gwin, gemb, gwd, gwd_s, gwd_r, gwd_all, gwin_s, gwin_r, gwin_all,
    recvB, epart, esend, erecv, eall,
    lsem, ids_s, ids_r, win_s2, win_r2, bias_s, bias_r, wdy_s, wdy_r, wdc_s, wdc_r, wz_s, wz_r, wx_s, wx_r, wc_s, wc_r,
    xp_s, xp_r, f_s, f_r, stp_s, stp_r, lgp_s, lgp_r, b_s, b_r, pgx_s, pgx_r,
    gwd_sems, gwin_sems, B_s, B_r, C_s, C_r, e_s, e_r,
):
    R, RR, Hy, U, U2, NR, L, VP = dims.R, dims.RR, dims.Hy, dims.U, dims.U2, dims.NR, dims.L, dims.VP
    KR, EW, V8, VS, RL, RB, QN = dims.KR, dims.EW, dims.V8, dims.VS, dims.RL, dims.RB, dims.QN
    peers = dims.peers
    pieces = 4 // QN
    rho, hid = lax.axis_index("rows"), lax.axis_index("hid")
    d, g, r = rho // (R // 2), lax.rem(rho // RR, 2), lax.rem(rho, RR)
    y, c = hid // 2, lax.rem(hid, 2)
    mine = y * 2 + g
    part = d * 2 + g

    def dev(dd, gg, rr, yy, cc):
        return (dd * (R // 2) + gg * RR + rr, yy * 2 + cc)

    def copy_to(src, dst, send, recv, device):
        return pltpu.make_async_remote_copy(
            src_ref=src, dst_ref=dst, send_sem=send, recv_sem=recv, device_id=device, device_id_type=MESH
        )

    def add_r(step):
        return lax.rem(r + step, RR)

    def add_y(step):
        return lax.rem(y + step, Hy)

    def rows_of(dd, gg, rr):
        index = dd * (R // 2) + gg * RR + rr
        per = U // KR
        block = index // per
        hid_of, g_of = block // 2, lax.rem(block, 2)
        chip = (hid_of // 2) * 2 + g_of
        row = chip * U2 + lax.rem(hid_of, 2) * U + lax.rem(index, per) * KR
        return pl.ds(pl.multiple_of(row, KR), KR)

    def chip_rows(m):
        return pl.ds(pl.multiple_of(m * U2, U2), U2)

    partner = dev(d, g, r, y, 1 - c)
    half = pl.ds(pl.multiple_of(g * U, U), U)

    def z_dev(j):
        return dev(flip(d, Z_STEPS[j][0]), flip(g, Z_STEPS[j][1]), r, y, c)

    def r_dev(step):
        return dev(d, g, add_r(step), y, c)

    def y_dev(step):
        return dev(d, g, r, add_y(step), c)

    def peer_dev(p):
        return dev(d, flip(g, peers[p][0]), r, add_y(peers[p][1]), c)

    barrier = pltpu.get_barrier_semaphore()
    greeted = [z_dev(j) for j in range(3)] + [r_dev(k) for k in range(1, RR)] + [partner]
    greeted += [peer_dev(p) for p in range(len(peers)) if peers[p] != (1, 0)]
    for device in greeted:
        pl.semaphore_signal(barrier, inc=1, device_id=device, device_id_type=MESH)
    pl.semaphore_wait(barrier, len(greeted))

    def ids_copy(j):
        return copy_to(idsrc.at[flip(d, Z_STEPS[j][0])], idsall.at[part], ids_s.at[j], ids_r.at[j], z_dev(j))

    def gates_of(n):
        return pl.ds(n * QN, QN)

    def wz_copy(j, n):
        columns = pl.ds(pl.multiple_of(flip(g, Z_STEPS[j][1]) * U, U), U)
        there = wrec_in.at[flip(d, Z_STEPS[j][0]), gates_of(n), :, columns]
        return copy_to(there, W.at[c, gates_of(n), rows_of(d, g, r), :], wz_s.at[j, n], wz_r.at[j, n], z_dev(j))

    def z_block(j):
        steps = Z_STEPS[j] if j < 3 else (0, 0)
        return flip(d, steps[0]), flip(g, steps[1])

    def w_block(core, j, k, n):
        dd, gg = z_block(j)
        return W.at[core, gates_of(n), rows_of(dd, gg, lax.rem(r + RR - k, RR)), :]

    def wx_copy(j, k, n):
        block = w_block(c, j, 0, n)
        return copy_to(block, block, wx_s.at[j, k - 1, n], wx_r.at[j, k - 1, n], r_dev(k))

    def wc_copy(j, k, n, core):
        block = w_block(core, j, k, n)
        return copy_to(block, block, wc_s.at[j, k, n], wc_r.at[j, k, n], partner)

    def wd_rows(yy):
        return wd.at[pl.ds(yy * 2, 2), c]

    def wdy_copy(k):
        return copy_to(wdec_in.at[d], wd_rows(y), wdy_s.at[k - 1], wdy_r.at[k - 1], y_dev(k))

    def wdc_copy(k):
        yy = lax.rem(y + Hy - k, Hy)
        return copy_to(wd_rows(yy), wd_rows(yy), wdc_s.at[k], wdc_r.at[k], partner)

    win_copy = copy_to(win_in.at[d, :, :, half], win.at[c], win_s2.at[0], win_r2.at[0], partner)
    bias_copy = copy_to(bias.at[c], bias.at[c], bias_s.at[0], bias_r.at[0], partner)
    own_win = pltpu.make_async_copy(win_in.at[d, :, :, half], win.at[c], lsem.at[1])
    own_wd = pltpu.make_async_copy(wdec_in.at[d], wd_rows(y), lsem.at[2])
    own_w = pltpu.make_async_copy(
        wrec_in.at[d, :, :, half], W.at[c, :, rows_of(d, g, r), :], lsem.at[3]
    )

    own_w.start()
    for n in range(pieces):
        for j in range(3):
            wz_copy(j, n).start()
    own_win.start()
    win_copy.start()
    for k in range(1, Hy):
        wdy_copy(k).start()
    own_wd.start()

    P8 = dims.P8
    idsrc[...] = jnp.zeros_like(idsrc)
    for dd in range(2):
        idsrc[dd, 0:L, 0:RL] = chars_ref[...].astype(F32)
        idsrc[dd, P8 : P8 + L, 0:RL] = targets_ref[dd].astype(F32)
        idsrc[dd, 2 * P8 : 2 * P8 + 8, 0:RL] = jnp.broadcast_to(lang_ref[...].astype(F32), (8, RL))
    for j in range(3):
        ids_copy(j).start()
    bias[c, 0:4] = bias_ref[d, :, half]
    bias_copy.start()
    idsall[part] = idsrc[d]

    own_w.wait()
    for n in range(pieces):
        for k in range(1, RR):
            wx_copy(3, k, n).start()
        wc_copy(3, 0, n, c).start()

    dW[...] = jnp.zeros_like(dW)
    gwin[...] = jnp.zeros_like(gwin)
    gemb[...] = jnp.zeros_like(gemb)
    lossv[...] = jnp.zeros_like(lossv)
    gb[...] = jnp.zeros_like(gb)
    cg[...] = jnp.zeros_like(cg)
    cell[0] = jnp.zeros_like(cell[0])
    idtmp[...] = jnp.zeros_like(idtmp)

    for j in range(3):
        ids_copy(j).wait_recv()
    for n in range(4):
        idtmp[:, 0 : idsall.shape[1]] = idsall[n].T
        ids[n] = idtmp[pl.ds(pl.multiple_of(c * (RL // 2), RL // 2), RL // 2), :]

    lane = lax.broadcasted_iota(jnp.int32, (NR, 128), 1)
    vocab = lax.broadcasted_iota(jnp.int32, (NR, VP), 1).astype(F32)

    def id_column(at):
        held = ids[...].reshape(NR, 128)
        return jnp.sum(jnp.where(lane == at, held, 0.0), axis=1, keepdims=True)

    def place(t):
        return t + d * (L - 1 - 2 * t)

    def char_hot(t):
        return jnp.where(vocab == id_column(place(t)), 1.0, 0.0).astype(BF16)

    lang_lane = lax.broadcasted_iota(jnp.int32, (NR, mask_ref.shape[0]), 1).astype(F32)
    lang_hot = jnp.where(lang_lane == id_column(2 * P8), 1.0, 0.0).astype(BF16)
    allowed[...] = dot(lang_hot, mask_ref[...])

    @pl.loop(0, L)
    def _(t):
        x[t] = dot(char_hot(t), emb_ref[d]).astype(BF16)

    xp_copy = copy_to(x, xp, xp_s.at[0], xp_r.at[0], partner)
    xp_copy.start()

    own_wd.wait()
    wdc_copy(0).start()
    own_win.wait()
    win_copy.wait_recv()
    bias_copy.wait_recv()

    def part_rows(b):
        return pl.ds(b * RB, RB)

    def f_copy(t, b, p):
        slot = lax.rem(t, 2)
        block = st.at[t, mine, part_rows(b), :]
        return copy_to(block, block, f_s.at[slot, b, p], f_r.at[slot, b, p], peer_dev(p))

    def gates(t, b):
        rows = part_rows(b)
        for cc in range(2):
            si = jax.nn.sigmoid(acc[cc, 0])
            sf = jax.nn.sigmoid(acc[cc, 1])
            tg = jnp.tanh(acc[cc, 2])
            so = jax.nn.sigmoid(acc[cc, 3])
            new = sf * cell[t, cc, rows] + si * tg
            cell[t + 1, cc, rows] = new
            st[t, mine, rows, cc * U : (cc + 1) * U] = (so * jnp.tanh(new)).astype(BF16)
            gs[t, 0, cc, rows] = si
            gs[t, 1, cc, rows] = sf
            gs[t, 2, cc, rows] = tg
            gs[t, 3, cc, rows] = so

    def peer_block(p):
        yy = lax.rem(y + Hy - peers[p][1], Hy)
        return yy * 2 + flip(g, peers[p][0])

    for b in range(BATCHES):
        for cc in range(2):
            for q in range(4):
                acc[cc, q] = dot(x[0, part_rows(b)], win[cc, q]) + bias[cc, q : q + 1]
        gates(0, b)
        for p in range(len(peers)):
            f_copy(0, b, p).start()

    for k in range(1, Hy):
        wdy_copy(k).wait_recv()
        wdc_copy(k).start()
    from_z = [(j, n) for n in range(pieces) for j in (2, 0, 1)]
    from_x = [(3, n) for n in range(pieces)] + from_z
    for at in range(len(from_x)):
        if at < len(from_z):
            j, n = from_z[at]
            wz_copy(j, n).wait_recv()
            for k in range(1, RR):
                wx_copy(j, k, n).start()
            wc_copy(j, 0, n, c).start()
        j, n = from_x[at]
        for k in range(1, RR):
            wx_copy(j, k, n).wait_recv()
            wc_copy(j, k, n, c).start()
    for j, n in from_x:
        for k in range(RR):
            wc_copy(j, k, n, 1 - c).wait_recv()
    for k in range(Hy):
        yy = lax.rem(y + Hy - k, Hy)
        other = wd.at[pl.ds(yy * 2, 2), 1 - c]
        copy_to(other, other, wdc_s.at[k], wdc_r.at[k], partner).wait_recv()

    def stp_copy(t):
        return copy_to(st.at[t], stp.at[t], stp_s.at[t], stp_r.at[t], partner)

    def lgp_copy(t):
        return copy_to(lg.at[t], lgp.at[t], lgp_s.at[t], lgp_r.at[t], partner)

    def decode(t):
        stp_copy(t).start()
        logits = bdec_ref[d]
        for m in range(2 * Hy):
            logits = logits + dot(st[t, m], wd[m].reshape(U2, VP))
        masked = jnp.where(allowed[...] > 0.5, logits, masked_value)
        top = jnp.max(masked, axis=1, keepdims=True)
        powers = jnp.exp(masked - top)
        total = jnp.sum(powers, axis=1, keepdims=True)
        hot = vocab == id_column(P8 + place(t))
        picked = jnp.sum(jnp.where(hot, logits, 0.0), axis=1, keepdims=True)
        lossv[...] += jnp.broadcast_to(top + jnp.log(total) - picked, (NR, 128))
        grad = ((powers / total - jnp.where(hot, 1.0, 0.0)) * dims.scale).astype(BF16)
        lg[t] = grad
        gb[0:1, :] += jnp.sum(grad.astype(F32), axis=0, keepdims=True)
        lgp_copy(t).start()

    @pl.loop(1, L)
    def _(t):
        for b in range(BATCHES):
            rows = part_rows(b)
            for cc in range(2):
                for q in range(4):
                    start = dot(x[t, rows], win[cc, q]) + bias[cc, q : q + 1]
                    acc[cc, q] = start + dot(st[t - 1, mine, rows], W[cc, q, chip_rows(mine), :])
            for p in reversed(range(len(peers))):
                f_copy(t - 1, b, p).wait_recv()
                m = peer_block(p)
                for cc in range(2):
                    for q in range(4):
                        acc[cc, q] += dot(st[t - 1, m, rows], W[cc, q, chip_rows(m), :])
            gates(t, b)
            for p in range(len(peers)):
                f_copy(t - 1, b, p).wait_send()
            for p in range(len(peers)):
                f_copy(t, b, p).start()
        decode(t - 1)

    for j, n in from_x:
        if j < 3:
            wz_copy(j, n).wait_send()
        for k in range(1, RR):
            wx_copy(j, k, n).wait_send()
        for k in range(RR):
            wc_copy(j, k, n, c).wait_send()

    @pl.loop(0, dims.H // U)
    def _(k):
        rows = pl.ds(pl.multiple_of(k * U, U), U)
        for cc in range(2):
            for q in range(4):
                W[cc, q, rows, :] = W[cc, q, rows, :].T

    for b in range(BATCHES):
        for p in reversed(range(len(peers))):
            f_copy(L - 1, b, p).wait_recv()
    decode(L - 1)

    def dec_back(t, cc):
        return dot_nt(lg[t], wd[mine, cc])

    def b_copy(t, b, p):
        slot = lax.rem(t, 2)
        there = precv.at[slot, p, part_rows(b), :]
        return copy_to(
            psend.at[slot, p, part_rows(b), :], there, b_s.at[slot, b, p], b_r.at[slot, b, p], peer_dev(p)
        )

    def pgx_copy(t):
        slot = lax.rem(t, 2)
        return copy_to(pg.at[slot, 1 - c], pgx.at[slot], pgx_s.at[slot], pgx_r.at[slot], partner)

    def preact_grads(t, b):
        slot = lax.rem(t, 2)
        rows = part_rows(b)
        for cc in range(2):
            h = dh[cc, rows]
            si, sf, tg, so = (gs[t, q, cc, rows] for q in range(4))
            tc = jnp.tanh(cell[t + 1, cc, rows])
            total = cg[cc, rows] + h * so * (1.0 - tc * tc)
            pg[slot, cc, 0, rows] = (total * tg * si * (1.0 - si)).astype(BF16)
            pg[slot, cc, 1, rows] = (total * cell[t, cc, rows] * sf * (1.0 - sf)).astype(BF16)
            pg[slot, cc, 2, rows] = (total * si * (1.0 - tg * tg)).astype(BF16)
            pg[slot, cc, 3, rows] = (h * tc * so * (1.0 - so)).astype(BF16)
            cg[cc, rows] = total * sf

    def partial(t, b, m, cc):
        slot = lax.rem(t, 2)
        rows = pl.ds(pl.multiple_of(m * U2 + cc * U, U), U)
        total = None
        for kk in range(2):
            for q in range(4):
                term = dot(pg[slot, kk, q, part_rows(b)], W[kk, q, rows, :])
                total = term if total is None else total + term
        return total

    def take_state_grad(t, b):
        slot = lax.rem(t, 2)
        rows = part_rows(b)
        for p in reversed(range(len(peers))):
            b_copy(t, b, p).wait_recv()
            for cc in range(2):
                dh[cc, rows] += precv[slot, p, rows, cc * U : (cc + 1) * U].astype(F32)

    def weight_grads(t, with_rec):
        slot = lax.rem(t, 2)
        pgx_copy(t).wait_recv()
        for q in range(4):
            both = jnp.concatenate([pg[slot, c, q], pgx[slot, q]], axis=0)
            gwin[q] += dot_tn(jnp.concatenate([x[t], xp[t]], axis=0), both)
            if with_rec:
                for m in range(2 * Hy):
                    states = jnp.concatenate([st[t - 1, m], stp[t - 1, m]], axis=0)
                    dW[q, m * U2 : (m + 1) * U2, :] += dot_tn(states, both)
        back = None
        for cc in range(2):
            for q in range(4):
                term = dot_nt(pg[slot, cc, q], win[cc, q])
                back = term if back is None else back + term
        high = back.astype(BF16)
        rest = (back - high.astype(F32)).astype(BF16)
        hot = char_hot(t)
        gemb[...] += dot_tn(hot, high) + dot_tn(hot, rest)

    class SmallSum:
        def __init__(self, send, recv, whole, out, sems, own_sem):
            self.send, self.recv, self.whole, self.out, self.sems, self.own = send, recv, whole, out, sems, own_sem
            self.share = whole.shape[1] // RR

        def rows(self, rr):
            return pl.ds(pl.multiple_of(rr * self.share, 16), self.share)

        def pair(self, at):
            return self.sems.at[0, at], self.sems.at[1, at]

        def first(self, k):
            return copy_to(self.send.at[self.rows(add_r(k)), :], self.recv.at[k - 1], *self.pair(k - 1), r_dev(k))

        def block(self, dd, gg):
            return self.whole.at[dd, self.rows(r), pl.ds(pl.multiple_of(gg * U, U), U)]

        def along(self, j):
            block = self.block(1 - d, g) if j == 1 else self.block(d, g)
            return copy_to(block, block, *self.pair(RR - 1 + j), z_dev(0 if j == 0 else 2))

        def last(self, k):
            block = self.whole.at[:, self.rows(r), :]
            return copy_to(block, block, *self.pair(RR + 2 + k - 1), r_dev(k))

        def to_out(self):
            return pltpu.make_async_copy(self.whole, self.out, self.own)

        def start(self):
            for k in range(1, RR):
                self.first(k).start()

        def add(self, value):
            for k in range(1, RR):
                self.first(k).wait_recv()
                value = value + self.recv[k - 1].astype(F32)
            self.whole[d, self.rows(r), half] = value.astype(BF16)
            self.along(0).start()
            self.along(2).start()

        def relay(self):
            self.along(0).wait_recv()
            self.along(1).start()

        def spread(self):
            self.along(2).wait_recv()
            self.along(1).wait_recv()
            for k in range(1, RR):
                self.last(k).start()

        def finish(self):
            for k in range(1, RR):
                self.last(k).wait_recv()
            self.to_out().start()

        def drain(self):
            for k in range(1, RR):
                self.first(k).wait_send()
                self.last(k).wait_send()
            for j in range(3):
                self.along(j).wait_send()
            self.to_out().wait()

    dec_sum = SmallSum(gwd_s, gwd_r, gwd_all, gwd_out, gwd_sems, lsem.at[0])
    in_sum = SmallSum(gwin_s, gwin_r, gwin_all, gwin_out, gwin_sems, lsem.at[1])

    def decoder_grad():
        gwd[...] = jnp.zeros_like(gwd)

        @pl.loop(0, L)
        def _(t):
            columns = pl.ds(pl.multiple_of(c * U, U), U)
            states = jnp.concatenate([st[t, mine, :, columns], stp[t, mine, :, columns]], axis=0)
            gwd[...] += dot_tn(jnp.concatenate([lg[t], lgp[t]], axis=0), states)

        gwd_s[...] = gwd[0 : dims.N_DEC].astype(BF16)
        dec_sum.start()

    for cc in range(2):
        dh[cc] = dec_back(L - 1, cc)

    @pl.loop(0, L)
    def _(t):
        stp_copy(t).wait()
        lgp_copy(t).wait()

    xp_copy.wait()

    @pl.loop(0, L - 1)
    def _(i):
        t = L - 1 - i
        slot = lax.rem(t, 2)

        @pl.when(i > 1)
        def _():
            pgx_copy(t + 2).wait_send()

        for b in range(BATCHES):
            rows = part_rows(b)

            @pl.when(i > 0)
            def _():
                take_state_grad(t + 1, b)

            @pl.when(i > 1)
            def _():
                for p in range(len(peers)):
                    b_copy(t + 2, b, p).wait_send()

            preact_grads(t, b)
            for p in range(len(peers)):
                m = add_y(peers[p][1]) * 2 + flip(g, peers[p][0])
                for cc in range(2):
                    psend[slot, p, rows, cc * U : (cc + 1) * U] = partial(t, b, m, cc).astype(BF16)
                b_copy(t, b, p).start()
            for cc in range(2):
                dh[cc, rows] = partial(t, b, mine, cc)
        pgx_copy(t).start()
        for cc in range(2):
            dh[cc] += dec_back(t - 1, cc)
        weight_grads(t, True)

        @pl.when(i == 0)
        def _():
            decoder_grad()

        @pl.when(i == 1)
        def _():
            dec_sum.add(gwd[dec_sum.rows(r), :])

        @pl.when(i == 2)
        def _():
            dec_sum.relay()

        @pl.when(i == 3)
        def _():
            dec_sum.spread()

        @pl.when(i == 4)
        def _():
            dec_sum.finish()

    out_steps = ((1, 0), (1, 1), (0, 1), (0, 0))

    def out_rows(i, step):
        dd, gg = flip(d, out_steps[i][0]), flip(g, out_steps[i][1])
        return rows_of(dd, gg, add_r(step))

    def b_out(i, k, n):
        return copy_to(
            W.at[0, gates_of(n), out_rows(i, k), :], recvB.at[k - 1, i, gates_of(n)],
            B_s.at[k - 1, i, n], B_r.at[k - 1, i, n], r_dev(k),
        )

    def c_out(i, n):
        there = grec_out.at[d, gates_of(n), :, half]
        return copy_to(W.at[1, gates_of(n), out_rows(i, 0), :], there, C_s.at[i, n], C_r.at[i, n], z_dev(i))

    def own_out(n):
        there = grec_out.at[d, gates_of(n), :, half]
        return pltpu.make_async_copy(W.at[1, gates_of(n), out_rows(3, 0), :], there, C_s.at[3, n])

    steps = [(i, n) for i in range(4) for n in range(pieces)]

    def send_over(at):
        i, n = steps[at]
        for k in range(1, RR):
            for q in range(n * QN, (n + 1) * QN):
                W[0, q, out_rows(i, k), :] = dW[q, out_rows(i, k), :].astype(BF16)
            b_out(i, k, n).start()

    def send_home(at):
        i, n = steps[at]
        for k in range(1, RR):
            b_out(i, k, n).wait_recv()
        for q in range(n * QN, (n + 1) * QN):
            total = dW[q, out_rows(i, 0), :]
            for k in range(1, RR):
                total = total + recvB[k - 1, i, q].astype(F32)
            W[1, q, out_rows(i, 0), :] = total.astype(BF16)
        if i < 3:
            c_out(i, n).start()
        else:
            own_out(n).start()

    ahead = min(AHEAD, len(steps))
    for at in range(ahead):
        send_over(at)

    pgx_copy(2).wait_send()
    for b in range(BATCHES):
        take_state_grad(1, b)
        preact_grads(0, b)
    pgx_copy(0).start()
    weight_grads(0, False)

    gwin_s[...] = jnp.zeros_like(gwin_s)
    for q in range(4):
        gwin_s[q * EW : (q + 1) * EW] = gwin[q, 0:EW].astype(BF16)
    in_sum.start()

    once = jnp.where(mine == 0, 1.0, 0.0).astype(F32)
    epart[0:V8] = gemb[0:V8]
    epart[V8:VS] = jnp.zeros((VS - V8, 128), F32)
    for k in range(VP // 128):
        epart[V8 + k : V8 + k + 1] = gb[0:1, k * 128 : (k + 1) * 128] * once
    at = V8 + VP // 128
    epart[at : at + 1] = jnp.sum(lossv[...], axis=0, keepdims=True) * (once * dims.scale)

    stages = [[partner], [r_dev(k) for k in range(1, RR)], [y_dev(k) for k in range(1, Hy)], [dev(d, 1 - g, r, y, c)]]
    first = [sum(len(s) for s in stages[:n]) for n in range(len(stages) + 1)]

    def e_half(core):
        return pl.ds(pl.multiple_of(core * (VS // 2), 8), VS // 2)

    def e_copy(n, k):
        at = first[n] + k
        there = epart.at[e_half(1 - c), :] if n == 0 else esend.at[n - 1]
        return copy_to(there, erecv.at[at], e_s.at[at], e_r.at[at], stages[n][k])

    def e_start(n):
        for k in range(len(stages[n])):
            e_copy(n, k).start()

    def e_take(n):
        total = epart[e_half(c), :] if n == 0 else esend[n - 1]
        for k in range(len(stages[n])):
            e_copy(n, k).wait_recv()
            total = total + erecv[first[n] + k]
        if n < 3:
            esend[n] = total
            e_start(n + 1)
        else:
            eall[d, e_half(c), :] = total
            e_cross.start()

    e_cross = copy_to(
        eall.at[d, e_half(c), :], eall.at[d, e_half(c), :], e_s.at[first[4]], e_r.at[first[4]], dev(1 - d, g, r, y, c)
    )
    e_core = copy_to(
        eall.at[:, e_half(c), :], eall.at[:, e_half(c), :], e_s.at[first[4] + 1], e_r.at[first[4] + 1], partner
    )
    own_small = pltpu.make_async_copy(eall, small_out, lsem.at[2])

    def in_share():
        in_f32 = jnp.concatenate([gwin[q, 0:EW] for q in range(4)], axis=0)
        if dims.N_IN > 4 * EW:
            in_f32 = jnp.concatenate([in_f32, jnp.zeros((dims.N_IN - 4 * EW, U), F32)], axis=0)
        share = in_sum.share
        total = in_f32[0:share]
        for k in range(1, RR):
            total = jnp.where(r == k, in_f32[k * share : (k + 1) * share], total)
        return total

    def e_gather():
        e_cross.wait_recv()
        e_core.start()

    def e_finish():
        e_core.wait_recv()
        own_small.start()

    e_start(0)
    between = [
        lambda: e_take(0), lambda: in_sum.add(in_share()), lambda: e_take(1), lambda: e_take(2), in_sum.relay,
        lambda: e_take(3), in_sum.spread, e_gather, in_sum.finish, e_finish,
    ]
    for at in range(len(steps)):
        send_home(at)
        if at + ahead < len(steps):
            send_over(at + ahead)
        if between:
            between.pop(0)()
    for event in between:
        event()

    for j in range(3):
        ids_copy(j).wait_send()
    win_copy.wait_send()
    bias_copy.wait_send()
    for k in range(1, Hy):
        wdy_copy(k).wait_send()
    for k in range(Hy):
        wdc_copy(k).wait_send()
    for b in range(BATCHES):
        for p in range(len(peers)):
            f_copy(L - 1, b, p).wait_send()
            b_copy(2, b, p).wait_send()
            b_copy(1, b, p).wait_send()
    pgx_copy(1).wait_send()
    pgx_copy(0).wait_send()
    for n in range(4):
        for k in range(len(stages[n])):
            e_copy(n, k).wait_send()
    e_cross.wait_send()
    e_core.wait_send()
    dec_sum.drain()
    in_sum.drain()
    for i, n in steps:
        for k in range(1, RR):
            b_out(i, k, n).wait_send()
        if i < 3:
            c_out(i, n).wait()
        else:
            own_out(n).wait()
    own_small.wait()


def call_kernel(dims, *operands):
    R, RR, Hy, U, U2, NR, L, VP = dims.R, dims.RR, dims.Hy, dims.U, dims.U2, dims.NR, dims.L, dims.VP
    KR, EP, VS, H, RB, N_IN, N_DEC = dims.KR, dims.EP, dims.VS, dims.H, dims.RB, dims.N_IN, dims.N_DEC
    chips, peers, pieces = 2 * Hy, len(dims.peers), 4 // dims.QN
    vmem, sem = pltpu.VMEM, pltpu.SemaphoreType.DMA
    apart = pl.BlockSpec(memory_space=pl.ANY)
    inside = pl.BlockSpec(memory_space=pltpu.VMEM)
    groups = max(RR - 1, 1)
    along = max(Hy - 1, 1)
    stages = 1 + (RR - 1) + (Hy - 1) + 1
    id_rows = 2 * dims.P8 + 8
    scratch = [
        vmem((2, id_rows, 128), F32),
        vmem((4, id_rows, 128), F32),
        vmem((128, 128), F32),
        vmem((4, dims.RL // 2, 128), F32),
        vmem((2, 8, U), F32),
        vmem((2, 4, EP, U), BF16),
        vmem((2, 4, H, U), BF16),
        vmem((chips, 2, U, VP), BF16),
        vmem((L, NR, EP), BF16),
        vmem((L, NR, EP), BF16),
        vmem((NR, VP), F32),
        vmem((2, 4, RB, U), F32),
        vmem((L, chips, NR, U2), BF16),
        vmem((L, chips, NR, U2), BF16),
        vmem((L, 4, 2, NR, U), F32),
        vmem((L + 1, 2, NR, U), F32),
        vmem((L, NR, VP), BF16),
        vmem((L, NR, VP), BF16),
        vmem((NR, 128), F32),
        vmem((8, VP), F32),
        vmem((2, NR, U), F32),
        vmem((2, NR, U), F32),
        vmem((2, 2, 4, NR, U), BF16),
        vmem((2, 4, NR, U), BF16),
        vmem((2, peers, NR, U2), BF16),
        vmem((2, peers, NR, U2), BF16),
        vmem((4, H, U), F32),
        vmem((4, EP, U), F32),
        vmem((VP, EP), F32),
        vmem((max(VP, N_DEC), U), F32),
        vmem((N_DEC, U), BF16),
        vmem((groups, N_DEC // RR, U), BF16),
        vmem((2, N_DEC, 2 * U), BF16),
        vmem((N_IN, U), BF16),
        vmem((groups, N_IN // RR, U), BF16),
        vmem((2, N_IN, 2 * U), BF16),
        vmem((groups, 4, 4, KR, U), BF16),
        vmem((VS, 128), F32),
        vmem((3, VS // 2, 128), F32),
        vmem((stages, VS // 2, 128), F32),
        vmem((2, VS, 128), F32),
        sem((4,)),
        sem((3,)), sem((3,)),
        sem((1,)), sem((1,)),
        sem((1,)), sem((1,)),
        sem((along,)), sem((along,)),
        sem((Hy,)), sem((Hy,)),
        sem((3, pieces)), sem((3, pieces)),
        sem((4, groups, pieces)), sem((4, groups, pieces)),
        sem((4, RR, pieces)), sem((4, RR, pieces)),
        sem((1,)), sem((1,)),
        sem((2, BATCHES, peers)), sem((2, BATCHES, peers)),
        sem((L,)), sem((L,)),
        sem((L,)), sem((L,)),
        sem((2, BATCHES, peers)), sem((2, BATCHES, peers)),
        sem((2,)), sem((2,)),
        sem((2, 2 * groups + 3)),
        sem((2, 2 * groups + 3)),
        sem((groups, 4, pieces)), sem((groups, 4, pieces)),
        sem((4, pieces)), sem((4, pieces)),
        sem((stages + 2,)), sem((stages + 2,)),
    ]
    rows = NR * L
    flops = 2 * rows * (3 * H * 8 * U + 3 * H * VP)
    return pl.pallas_call(
        functools.partial(kernel, dims),
        out_shape=(
            jax.ShapeDtypeStruct((2, 4, KR, 2 * U), BF16),
            jax.ShapeDtypeStruct((2, N_IN, 2 * U), BF16),
            jax.ShapeDtypeStruct((2, N_DEC, 2 * U), BF16),
            jax.ShapeDtypeStruct((2, VS, 128), F32),
        ),
        in_specs=[inside] * 4 + [apart] * 3 + [inside] * 3,
        out_specs=(apart, apart, apart, apart),
        scratch_shapes=scratch,
        cost_estimate=pl.CostEstimate(flops=flops, bytes_accessed=8 << 20, transcendentals=rows * U2 * 8),
        compiler_params=pltpu.CompilerParams(
            collective_id=0, has_side_effects=True, vmem_limit_bytes=62 << 20
        ),
        name="train_step",
    )(*operands)


def local(
    char_ids, lang_ids, vocab_masks, targets, embedding, w_in, w_rec, b_in, b_rec, w_dec, b_dec
):
    R, hid = lax.axis_size("rows"), lax.axis_size("hid")
    RL, L = char_ids.shape
    E, units = w_in.shape[1], w_in.shape[3]
    V = embedding.shape[1]
    KR = w_rec.shape[1]
    U = units // 2
    dims = Dims(
        R=R, RR=R // 4, Hy=hid // 2, H=units * hid, KR=KR, U=U, RL=RL, L=L, V=V, E=E,
        LANGS=vocab_masks.shape[0], scale=1.0 / (RL * R * L),
    )
    VP, EP, EW = dims.VP, dims.EP, dims.EW

    bias = b_in.astype(F32) + b_rec.astype(F32)
    win = jnp.pad(w_in.transpose(0, 2, 1, 3), ((0, 0), (0, 0), (0, EP - E), (0, 0)))
    wrec = w_rec.transpose(0, 2, 1, 3)
    wdec = jnp.pad(w_dec, ((0, 0), (0, 0), (0, VP - V))).reshape(2, 2, U, VP)
    emb = jnp.concatenate([embedding, jnp.ones((2, V, 1), BF16)], axis=2)
    emb = jnp.pad(emb, ((0, 0), (0, VP - V), (0, EP - E - 1)))
    bdec = jnp.pad(b_dec.astype(F32), ((0, 0), (0, VP - V)))[:, None, :]
    lang_rows = ceil_to(dims.LANGS, 16)
    mask = jnp.pad(vocab_masks.astype(BF16), ((0, lang_rows - dims.LANGS), (0, VP - V)))

    grec, gwin, gwd, small = call_kernel(
        dims, char_ids.T, targets.transpose(0, 2, 1), lang_ids[None], bias, win, wrec, wdec, emb, bdec, mask
    )

    grad_w_rec = grec.astype(F32).transpose(0, 2, 1, 3)
    gwin = gwin[:, : 4 * EW].reshape(2, 4, EW, units).astype(F32)
    grad_w_in = gwin[:, :, :E].transpose(0, 2, 1, 3)
    grad_bias = gwin[:, :, E]
    grad_w_dec = gwd[:, :V].astype(F32).transpose(0, 2, 1)
    V8 = dims.V8
    grad_embedding = small[:, :V, :E]
    grad_b_dec = small[:, V8 : V8 + VP // 128].reshape(2, VP)[:, :V]
    total_loss = jnp.sum(small[:, V8 + VP // 128, 0])
    return (
        total_loss,
        grad_embedding,
        grad_w_in,
        grad_w_rec,
        grad_bias,
        grad_bias,
        grad_w_dec,
        grad_b_dec,
    )


def solution(mesh):
    placed = (
        P("rows", None),
        P("rows"),
        P(),
        P(None, "rows", None),
        P(),
        P(None, None, None, "hid"),
        P(None, "rows", None, "hid"),
        P(None, None, "hid"),
        P(None, None, "hid"),
        P(None, "hid", None),
        P(),
    )
    return jax.shard_map(
        local,
        mesh=mesh,
        in_specs=placed,
        out_specs=(
            P(),
            P(),
            P(None, None, None, "hid"),
            P(None, "rows", None, "hid"),
            P(None, None, "hid"),
            P(None, None, "hid"),
            P(None, "hid", None),
            P(),
        ),
        check_vma=False,
    )
```

time: 337 us -> 291 us (0.86)
  Pallas kernels: 287 us -> 266 us
  local copies, waits for them, and re-layouts: 38.3 us -> 21.3 us
  other arithmetic: 9.4 us -> 3.34 us
    pallas_call x1, Pallas kernels: 287 us -> 266 us  [call_kernel(): pl.pallas_call(functools.partial(kernel, dims), out_shape=(jax.ShapeDtype...]
    convert_element_type x6 -> x0, local copies, waits for them, and re-layouts: 19.1 us -> none  [the longest x2 12.2 us: local(): grec.reshape(2, 2, 4, KR, U).transpose(0, 3, 2, 1, 4)]
    unnamed x26 -> x34, local copies, waits for them, and re-layouts: 8.5 us -> 15.9 us
    convert_element_type x5 -> x0, other arithmetic: 4.29 us -> none  [the longest x1 2.03 us: local(): grec.reshape(2, 2, 4, KR, U).transpose(0, 3, 2, 1, 4)]
    reshape x2 -> x0, local copies, waits for them, and re-layouts: 3.66 us -> none  [the longest x1 2.35 us: local(): wrec = w_rec.reshape(2, KR, 4, 2, U).transpose(0, 3, 2, 1, 4)]
where the time goes in v2:
time: 291 us
  Pallas kernels  266 us (91%)
  local copies, waits for them, and re-layouts  21.3 us (7%)
  other arithmetic  3.34 us (1%)
    pallas_call x1, Pallas kernels, call_kernel(): pl.pallas_call(functools.partial(kernel, dims), out_shape=(jax.ShapeDtype...  266 us
    unnamed x34, local copies, waits for them, and re-layouts  15.9 us

profile of v2, /device:TPU:0, one launch (start us, length us, event | category | flops | bytes accessed | tf_op | source)
XLA Modules:
  0.0 291.1 jit_solution(3704978990821645565)
XLA Ops:
  0.6 0.0 copy-start.2
  0.6 3.4 %copy.46 = bf16[2,256,4,512]{3,1,2,0:T(8,128)(2,1)} copy(bf16[2,256,4,512]{3,2,1,0:T(4,128)(2,1)} %param.17) | data formatting | bytes 4194304 | tf_op args[6]
  4.0 0.0 copy-done.2
  4.0 0.2 copy.48
  4.2 0.0 copy-start.5
  4.2 1.1 pad.22.win_in
  5.3 0.0 copy-start.10
  5.3 0.7 copy.39
  6.1 1.0 pad.23.clone
  7.1 0.7 fusion.2.emb_ref
  7.8 0.6 pad.26.mask_ref
  8.4 0.0 copy-done.9
  8.4 0.6 convert_add_fusion
  9.0 0.0 copy-done.10
  9.0 0.6 reshape.27.bdec_ref
  9.6 265.7 %train_step.1 = (bf16[2,4,256,512]{3,2,1,0:T(8,128)(2,1)}, bf16[2,448,512]{2,1,0:T(8,128)(2,1)}, bf16[2,288,512]{2,1,0:T(8,128)(2,1)}, f32[2,288,128]{2,1,0:T(8,128)}) custom-call(s32[8,64]{1,0:T(8,128)} %bitcast.44, s32[2,8,64]{2,1,0:T(8,128)} %bitcast.43, s32[1,64]{1,0:T(1,128)} %bitcast.45, f32[2,4,512]{2,1,0:T(4,128)} %bitcast.39, ...), custom_call_target="tpu_custom_call" | custom-call | flops 30601641984 | bytes 8388608 | tf_op jit(solution)/shard_map/train_step/pallas_call | solution.py:871
  275.3 1.1 slice.22
  276.4 0.9 copy.34
  277.2 0.9 slice.29
  278.1 0.0 copy-start.6
  278.1 0.7 slice_bitcast_fusion
  278.8 0.6 copy.50
  279.4 1.3 slice_reduce_fusion
  280.7 0.2 slice.28
  280.9 2.2 copy.47
  283.2 0.6 convert_bitcast_fusion
  283.7 0.0 copy-start.4
  283.7 4.7 %copy.35 = f32[2,256,4,512]{3,2,1,0:T(4,128)} copy(f32[2,256,4,512]{3,1,2,0:T(8,128)S(1)} %convert_bitcast_fusion) | data formatting | bytes 8388608
  288.5 0.0 copy-done.4
  288.5 0.1 convert_bitcast_fusion.1
  288.6 1.9 copy.36
  290.5 0.6 copy.52
  (17 shorter events, 0.1 us)
Async XLA Ops:
  0.6 3.4 %copy-start.2 = (bf16[2,100,4,512]{3,2,1,0:T(4,128)(2,1)S(1)}, bf16[2,100,4,512]{3,2,1,0:T(4,128)(2,1)}, u32[]{:S(2)}) copy-start(bf16[2,100,4,512]{3,2,1,0:T(4,128)(2,1)} %param.16) | copy-start | bytes 2457604
  4.0 1.2 copy-start.3
  4.2 2.8 copy-start.5
  5.3 2.5 copy-start.7
  5.3 3.1 %copy-start.8 = (bf16[2,4,512]{2,1,0:T(4,128)(2,1)S(1)}, bf16[2,4,512]{2,1,0:T(4,128)(2,1)}, u32[]{:S(2)}) copy-start(bf16[2,4,512]{2,1,0:T(4,128)(2,1)} %param.19) | copy-start | bytes 24580
  5.3 3.1 %copy-start.9 = (bf16[2,4,512]{2,1,0:T(4,128)(2,1)S(1)}, bf16[2,4,512]{2,1,0:T(4,128)(2,1)}, u32[]{:S(2)}) copy-start(bf16[2,4,512]{2,1,0:T(4,128)(2,1)} %param.18) | copy-start | bytes 24580
  5.3 3.7 %copy-start.10 = (bf16[2,275]{1,0:T(2,128)(2,1)S(1)}, bf16[2,275]{1,0:T(2,128)(2,1)}, u32[]{:S(2)}) copy-start(bf16[2,275]{1,0:T(2,128)(2,1)} %param.21) | copy-start | bytes 3304
  275.3 5.4 %copy-start = (bf16[2,448,512]{2,1,0:T(8,128)(2,1)S(1)}, bf16[2,448,512]{2,1,0:T(8,128)(2,1)}, u32[]{:S(2)}) copy-start(bf16[2,448,512]{2,1,0:T(8,128)(2,1)} %get-tuple-element.13) | copy-start | bytes 2752516
  278.1 12.4 %copy-start.6 = (f32[2,4,1,512]{3,1,0,2:T(4,128)}, f32[2,4,1,512]{3,1,0,2:T(4,128)S(1)}, u32[]{:S(2)}) copy-start(f32[2,4,1,512]{3,1,0,2:T(4,128)S(1)} %copy.49) | copy-start | bytes 49156
  280.9 2.2 copy-start.1
  283.7 4.7 %copy-start.4 = (bf16[2,288,512]{2,1,0:T(8,128)(2,1)S(1)}, bf16[2,288,512]{2,1,0:T(8,128)(2,1)}, u32[]{:S(2)}) copy-start(bf16[2,288,512]{2,1,0:T(8,128)(2,1)} %get-tuple-element.15) | copy-start | bytes 1769476

commit v3 on v2

--- a/solution.py
+++ b/solution.py
@@ -12,7 +12,10 @@
 F32 = jnp.float32
 BF16 = jnp.bfloat16
 masked_value = -1000000000.0
-AHEAD = 4
+ROW_PARTS = 2
+AHEAD = 8
+EARLY = 2
+WINDOW = 2
 BATCHES = 2
 
 
@@ -53,6 +56,18 @@
     @property
     def QN(self):
         return 1 if self.RR <= 2 else 4
+
+    @property
+    def KP(self):
+        return ROW_PARTS if self.RR <= 2 else 1
+
+    @property
+    def pieces(self):
+        return 4 // self.QN * self.KP
+
+    @property
+    def KRP(self):
+        return self.KR // self.KP
 
     @property
     def N_IN(self):
@@ -122,7 +137,7 @@
     R, RR, Hy, U, U2, NR, L, VP = dims.R, dims.RR, dims.Hy, dims.U, dims.U2, dims.NR, dims.L, dims.VP
     KR, EW, V8, VS, RL, RB, QN = dims.KR, dims.EW, dims.V8, dims.VS, dims.RL, dims.RB, dims.QN
     peers = dims.peers
-    pieces = 4 // QN
+    KP, KRP, pieces = dims.KP, dims.KRP, dims.pieces
     rho, hid = lax.axis_index("rows"), lax.axis_index("hid")
     d, g, r = rho // (R // 2), lax.rem(rho // RR, 2), lax.rem(rho, RR)
     y, c = hid // 2, lax.rem(hid, 2)
@@ -143,14 +158,22 @@
     def add_y(step):
         return lax.rem(y + step, Hy)
 
-    def rows_of(dd, gg, rr):
+    def place_of(dd, gg, rr):
         index = dd * (R // 2) + gg * RR + rr
         per = U // KR
         block = index // per
         hid_of, g_of = block // 2, lax.rem(block, 2)
-        chip = (hid_of // 2) * 2 + g_of
-        row = chip * U2 + lax.rem(hid_of, 2) * U + lax.rem(index, per) * KR
-        return pl.ds(pl.multiple_of(row, KR), KR)
+        return (hid_of // 2) * 2 + g_of, lax.rem(hid_of, 2) * U + lax.rem(index, per) * KR
+
+    def rows_of(dd, gg, rr, n=None):
+        chip, unit = place_of(dd, gg, rr)
+        row = chip * U2 + unit
+        if n is None:
+            return pl.ds(pl.multiple_of(row, KR), KR)
+        return pl.ds(pl.multiple_of(row + n % KP * KRP, KRP), KRP)
+
+    def rows_in(n):
+        return pl.ds(n % KP * KRP, KRP)
 
     def chip_rows(m):
         return pl.ds(pl.multiple_of(m * U2, U2), U2)
@@ -181,12 +204,12 @@
         return copy_to(idsrc.at[flip(d, Z_STEPS[j][0])], idsall.at[part], ids_s.at[j], ids_r.at[j], z_dev(j))
 
     def gates_of(n):
-        return pl.ds(n * QN, QN)
+        return pl.ds(n // KP * QN, QN)
 
     def wz_copy(j, n):
         columns = pl.ds(pl.multiple_of(flip(g, Z_STEPS[j][1]) * U, U), U)
-        there = wrec_in.at[flip(d, Z_STEPS[j][0]), gates_of(n), :, columns]
-        return copy_to(there, W.at[c, gates_of(n), rows_of(d, g, r), :], wz_s.at[j, n], wz_r.at[j, n], z_dev(j))
+        there = wrec_in.at[flip(d, Z_STEPS[j][0]), gates_of(n), rows_in(n), columns]
+        return copy_to(there, W.at[c, gates_of(n), rows_of(d, g, r, n), :], wz_s.at[j, n], wz_r.at[j, n], z_dev(j))
 
     def z_block(j):
         steps = Z_STEPS[j] if j < 3 else (0, 0)
@@ -194,7 +217,7 @@
 
     def w_block(core, j, k, n):
         dd, gg = z_block(j)
-        return W.at[core, gates_of(n), rows_of(dd, gg, lax.rem(r + RR - k, RR)), :]
+        return W.at[core, gates_of(n), rows_of(dd, gg, lax.rem(r + RR - k, RR), n), :]
 
     def wx_copy(j, k, n):
         block = w_block(c, j, 0, n)
@@ -223,7 +246,7 @@
     )
 
     own_w.start()
-    for n in range(pieces):
+    for n in range(min(WINDOW, pieces)):
         for j in range(3):
             wz_copy(j, n).start()
     own_win.start()
@@ -333,7 +356,9 @@
     for k in range(1, Hy):
         wdy_copy(k).wait_recv()
         wdc_copy(k).start()
-    from_z = [(j, n) for n in range(pieces) for j in (2, 0, 1)]
+    from_z, beside = [], [(2, n) for n in range(pieces)]
+    for n in range(pieces):
+        from_z += beside[2 * n : 2 * n + 2] + [(0, n), (1, n)]
     from_x = [(3, n) for n in range(pieces)] + from_z
     for at in range(len(from_x)):
         if at < len(from_z):
@@ -342,6 +367,8 @@
             for k in range(1, RR):
                 wx_copy(j, k, n).start()
             wc_copy(j, 0, n, c).start()
+            if n + WINDOW < pieces:
+                wz_copy(j, n + WINDOW).start()
         j, n = from_x[at]
         for k in range(1, RR):
             wx_copy(j, k, n).wait_recv()
@@ -429,8 +456,7 @@
         )
 
     def pgx_copy(t):
-        slot = lax.rem(t, 2)
-        return copy_to(pg.at[slot, 1 - c], pgx.at[slot], pgx_s.at[slot], pgx_r.at[slot], partner)
+        return copy_to(pg.at[lax.rem(t, 2), 1 - c], pgx.at[t], pgx_s.at[t], pgx_r.at[t], partner)
 
     def preact_grads(t, b):
         slot = lax.rem(t, 2)
@@ -464,16 +490,21 @@
             for cc in range(2):
                 dh[cc, rows] += precv[slot, p, rows, cc * U : (cc + 1) * U].astype(F32)
 
-    def weight_grads(t, with_rec):
+    def both_cores(t, q):
+        return jnp.concatenate([pg[lax.rem(t, 2), c, q], pgx[t, q]], axis=0)
+
+    def rec_grads(t):
+        for q in range(4):
+            both = both_cores(t, q)
+            for m in range(2 * Hy):
+                states = jnp.concatenate([st[t - 1, m], stp[t - 1, m]], axis=0)
+                dW[q, m * U2 : (m + 1) * U2, :] += dot_tn(states, both)
+
+    def in_grads(t):
         slot = lax.rem(t, 2)
-        pgx_copy(t).wait_recv()
+        inputs = jnp.concatenate([x[t], xp[t]], axis=0)
         for q in range(4):
-            both = jnp.concatenate([pg[slot, c, q], pgx[slot, q]], axis=0)
-            gwin[q] += dot_tn(jnp.concatenate([x[t], xp[t]], axis=0), both)
-            if with_rec:
-                for m in range(2 * Hy):
-                    states = jnp.concatenate([st[t - 1, m], stp[t - 1, m]], axis=0)
-                    dW[q, m * U2 : (m + 1) * U2, :] += dot_tn(states, both)
+            gwin[q] += dot_tn(inputs, both_cores(t, q))
         back = None
         for cc in range(2):
             for q in range(4):
@@ -604,7 +635,12 @@
         pgx_copy(t).start()
         for cc in range(2):
             dh[cc] += dec_back(t - 1, cc)
-        weight_grads(t, True)
+
+        @pl.when(i > 0)
+        def _():
+            pgx_copy(t + 1).wait_recv()
+            rec_grads(t + 1)
+            in_grads(t + 1)
 
         @pl.when(i == 0)
         def _():
@@ -628,57 +664,87 @@
 
     out_steps = ((1, 0), (1, 1), (0, 1), (0, 0))
 
-    def out_rows(i, step):
-        dd, gg = flip(d, out_steps[i][0]), flip(g, out_steps[i][1])
-        return rows_of(dd, gg, add_r(step))
+    def out_device(i, step):
+        return flip(d, out_steps[i][0]), flip(g, out_steps[i][1]), add_r(step)
+
+    def out_rows(i, step, n):
+        return rows_of(*out_device(i, step), n)
 
     def b_out(i, k, n):
         return copy_to(
-            W.at[0, gates_of(n), out_rows(i, k), :], recvB.at[k - 1, i, gates_of(n)],
+            W.at[0, gates_of(n), out_rows(i, k, n), :], recvB.at[k - 1, i, gates_of(n), rows_in(n), :],
             B_s.at[k - 1, i, n], B_r.at[k - 1, i, n], r_dev(k),
         )
 
     def c_out(i, n):
-        there = grec_out.at[d, gates_of(n), :, half]
-        return copy_to(W.at[1, gates_of(n), out_rows(i, 0), :], there, C_s.at[i, n], C_r.at[i, n], z_dev(i))
+        there = grec_out.at[d, gates_of(n), rows_in(n), half]
+        return copy_to(W.at[1, gates_of(n), out_rows(i, 0, n), :], there, C_s.at[i, n], C_r.at[i, n], z_dev(i))
 
     def own_out(n):
-        there = grec_out.at[d, gates_of(n), :, half]
-        return pltpu.make_async_copy(W.at[1, gates_of(n), out_rows(3, 0), :], there, C_s.at[3, n])
-
-    steps = [(i, n) for i in range(4) for n in range(pieces)]
+        there = grec_out.at[d, gates_of(n), rows_in(n), half]
+        return pltpu.make_async_copy(W.at[1, gates_of(n), out_rows(3, 0, n), :], there, C_s.at[3, n])
+
+    def gates_in(n):
+        return range(n // KP * QN, (n // KP + 1) * QN)
+
+    fused = KRP % 128 == 0
+
+    def rec_piece(i, step, n, q):
+        total = dW[q, out_rows(i, step, n), :]
+        if fused:
+            chip, unit = place_of(*out_device(i, step))
+            units = pl.ds(pl.multiple_of(unit + n % KP * KRP, 128), KRP)
+            states = jnp.concatenate([st[0, chip, :, units], stp[0, chip, :, units]], axis=0)
+            total = total + dot_tn(states, both_cores(1, q))
+        return total
+
+    steps = [(i, n) for n in range(pieces) for i in (0, 2, 1, 3)]
 
     def send_over(at):
         i, n = steps[at]
         for k in range(1, RR):
-            for q in range(n * QN, (n + 1) * QN):
-                W[0, q, out_rows(i, k), :] = dW[q, out_rows(i, k), :].astype(BF16)
+            for q in gates_in(n):
+                W[0, q, out_rows(i, k, n), :] = rec_piece(i, k, n, q).astype(BF16)
             b_out(i, k, n).start()
 
     def send_home(at):
         i, n = steps[at]
         for k in range(1, RR):
             b_out(i, k, n).wait_recv()
-        for q in range(n * QN, (n + 1) * QN):
-            total = dW[q, out_rows(i, 0), :]
+        for q in gates_in(n):
+            total = rec_piece(i, 0, n, q)
             for k in range(1, RR):
-                total = total + recvB[k - 1, i, q].astype(F32)
-            W[1, q, out_rows(i, 0), :] = total.astype(BF16)
+                total = total + recvB[k - 1, i, q, rows_in(n), :].astype(F32)
+            W[1, q, out_rows(i, 0, n), :] = total.astype(BF16)
         if i < 3:
             c_out(i, n).start()
         else:
             own_out(n).start()
-
+        if at + ahead < len(steps):
+            send_over(at + ahead)
+
+    pgx_copy(1).wait_recv()
+    if not fused:
+        rec_grads(1)
     ahead = min(AHEAD, len(steps))
     for at in range(ahead):
         send_over(at)
+    in_grads(1)
 
     pgx_copy(2).wait_send()
+    sent = 0
     for b in range(BATCHES):
         take_state_grad(1, b)
         preact_grads(0, b)
+        for at in range(sent, min(sent + EARLY, len(steps))):
+            send_home(at)
+        sent = min(sent + EARLY, len(steps))
     pgx_copy(0).start()
-    weight_grads(0, False)
+    for at in range(sent, min(sent + EARLY, len(steps))):
+        send_home(at)
+    sent = min(sent + EARLY, len(steps))
+    pgx_copy(0).wait_recv()
+    in_grads(0)
 
     gwin_s[...] = jnp.zeros_like(gwin_s)
     for q in range(4):
@@ -693,7 +759,7 @@
     at = V8 + VP // 128
     epart[at : at + 1] = jnp.sum(lossv[...], axis=0, keepdims=True) * (once * dims.scale)
 
-    stages = [[partner], [r_dev(k) for k in range(1, RR)], [y_dev(k) for k in range(1, Hy)], [dev(d, 1 - g, r, y, c)]]
+    stages = [[partner], [peer_dev(p) for p in range(len(peers))], [r_dev(k) for k in range(1, RR)]]
     first = [sum(len(s) for s in stages[:n]) for n in range(len(stages) + 1)]
 
     def e_half(core):
@@ -713,7 +779,7 @@
         for k in range(len(stages[n])):
             e_copy(n, k).wait_recv()
             total = total + erecv[first[n] + k]
-        if n < 3:
+        if n < 2:
             esend[n] = total
             e_start(n + 1)
         else:
@@ -721,10 +787,10 @@
             e_cross.start()
 
     e_cross = copy_to(
-        eall.at[d, e_half(c), :], eall.at[d, e_half(c), :], e_s.at[first[4]], e_r.at[first[4]], dev(1 - d, g, r, y, c)
+        eall.at[d, e_half(c), :], eall.at[d, e_half(c), :], e_s.at[first[3]], e_r.at[first[3]], z_dev(0)
     )
     e_core = copy_to(
-        eall.at[:, e_half(c), :], eall.at[:, e_half(c), :], e_s.at[first[4] + 1], e_r.at[first[4] + 1], partner
+        eall.at[:, e_half(c), :], eall.at[:, e_half(c), :], e_s.at[first[3] + 1], e_r.at[first[3] + 1], partner
     )
     own_small = pltpu.make_async_copy(eall, small_out, lsem.at[2])
 
@@ -748,16 +814,21 @@
 
     e_start(0)
     between = [
-        lambda: e_take(0), lambda: in_sum.add(in_share()), lambda: e_take(1), lambda: e_take(2), in_sum.relay,
-        lambda: e_take(3), in_sum.spread, e_gather, in_sum.finish, e_finish,
+        (0.05, lambda: e_take(0)),
+        (0.2, lambda: in_sum.add(in_share())),
+        (0.2, lambda: e_take(1)),
+        (0.35, lambda: e_take(2)),
+        (0.5, in_sum.relay),
+        (0.6, e_gather),
+        (0.7, in_sum.spread),
+        (0.8, e_finish),
+        (1.0, in_sum.finish),
     ]
-    for at in range(len(steps)):
+    for at in range(sent, len(steps)):
         send_home(at)
-        if at + ahead < len(steps):
-            send_over(at + ahead)
-        if between:
-            between.pop(0)()
-    for event in between:
+        while between and (at + 1 - sent) >= between[0][0] * (len(steps) - sent):
+            between.pop(0)[1]()
+    for _, event in between:
         event()
 
     for j in range(3):
@@ -775,7 +846,7 @@
             b_copy(1, b, p).wait_send()
     pgx_copy(1).wait_send()
     pgx_copy(0).wait_send()
-    for n in range(4):
+    for n in range(3):
         for k in range(len(stages[n])):
             e_copy(n, k).wait_send()
     e_cross.wait_send()
@@ -795,13 +866,13 @@
 def call_kernel(dims, *operands):
     R, RR, Hy, U, U2, NR, L, VP = dims.R, dims.RR, dims.Hy, dims.U, dims.U2, dims.NR, dims.L, dims.VP
     KR, EP, VS, H, RB, N_IN, N_DEC = dims.KR, dims.EP, dims.VS, dims.H, dims.RB, dims.N_IN, dims.N_DEC
-    chips, peers, pieces = 2 * Hy, len(dims.peers), 4 // dims.QN
+    chips, peers, pieces = 2 * Hy, len(dims.peers), dims.pieces
     vmem, sem = pltpu.VMEM, pltpu.SemaphoreType.DMA
     apart = pl.BlockSpec(memory_space=pl.ANY)
     inside = pl.BlockSpec(memory_space=pltpu.VMEM)
     groups = max(RR - 1, 1)
     along = max(Hy - 1, 1)
-    stages = 1 + (RR - 1) + (Hy - 1) + 1
+    stages = 1 + peers + (RR - 1)
     id_rows = 2 * dims.P8 + 8
     scratch = [
         vmem((2, id_rows, 128), F32),
@@ -827,7 +898,7 @@
         vmem((2, NR, U), F32),
         vmem((2, NR, U), F32),
         vmem((2, 2, 4, NR, U), BF16),
-        vmem((2, 4, NR, U), BF16),
+        vmem((L, 4, NR, U), BF16),
         vmem((2, peers, NR, U2), BF16),
         vmem((2, peers, NR, U2), BF16),
         vmem((4, H, U), F32),
@@ -842,7 +913,7 @@
         vmem((2, N_IN, 2 * U), BF16),
         vmem((groups, 4, 4, KR, U), BF16),
         vmem((VS, 128), F32),
-        vmem((3, VS // 2, 128), F32),
+        vmem((2, VS // 2, 128), F32),
         vmem((stages, VS // 2, 128), F32),
         vmem((2, VS, 128), F32),
         sem((4,)),
@@ -859,7 +930,7 @@
         sem((L,)), sem((L,)),
         sem((L,)), sem((L,)),
         sem((2, BATCHES, peers)), sem((2, BATCHES, peers)),
-        sem((2,)), sem((2,)),
+        sem((L,)), sem((L,)),
         sem((2, 2 * groups + 3)),
         sem((2, 2 * groups + 3)),
         sem((groups, 4, pieces)), sem((groups, 4, pieces)),

time: 291 us -> 255 us (0.88)
  Pallas kernels: 266 us -> 229 us
    pallas_call x1, Pallas kernels: 266 us -> 229 us  [call_kernel(): pl.pallas_call(functools.partial(kernel, dims), out_shape=(jax.ShapeDtype...]
where the time goes in v3:
time: 255 us
  Pallas kernels  229 us (90%)
  local copies, waits for them, and re-layouts  21.3 us (8%)
  other arithmetic  3.34 us (1%)
    pallas_call x1, Pallas kernels, call_kernel(): pl.pallas_call(functools.partial(kernel, dims), out_shape=(jax.ShapeDtype...  229 us
    unnamed x34, local copies, waits for them, and re-layouts  15.9 us

profile of v3, /device:TPU:0, one launch (start us, length us, event | category | flops | bytes accessed | tf_op | source)
XLA Modules:
  0.0 254.7 jit_solution(10496415605779478513)
XLA Ops:
  0.6 0.0 copy-start.2
  0.6 3.4 %copy.46 = bf16[2,256,4,512]{3,1,2,0:T(8,128)(2,1)} copy(bf16[2,256,4,512]{3,2,1,0:T(4,128)(2,1)} %param.17) | data formatting | bytes 4194304 | tf_op args[6]
  4.0 0.0 copy-done.2
  4.0 0.2 copy.48
  4.2 0.0 copy-start.5
  4.2 1.1 pad.22.win_in
  5.3 0.0 copy-done.3
  5.3 0.0 copy-start.10
  5.3 0.7 copy.39
  6.1 1.0 pad.23.clone
  7.1 0.7 fusion.2.emb_ref
  7.8 0.6 pad.26.mask_ref
  8.4 0.0 copy-done.9
  8.4 0.6 convert_add_fusion
  9.0 0.6 reshape.27.bdec_ref
  9.6 229.3 %train_step.1 = (bf16[2,4,256,512]{3,2,1,0:T(8,128)(2,1)}, bf16[2,448,512]{2,1,0:T(8,128)(2,1)}, bf16[2,288,512]{2,1,0:T(8,128)(2,1)}, f32[2,288,128]{2,1,0:T(8,128)}) custom-call(s32[8,64]{1,0:T(8,128)} %bitcast.44, s32[2,8,64]{2,1,0:T(8,128)} %bitcast.43, s32[1,64]{1,0:T(1,128)} %bitcast.45, f32[2,4,512]{2,1,0:T(4,128)} %bitcast.39, ...), custom_call_target="tpu_custom_call" | custom-call | flops 30601641984 | bytes 8388608 | tf_op jit(solution)/shard_map/train_step/pallas_call | solution.py:942
  239.0 1.1 slice.22
  240.0 0.9 copy.34
  240.9 0.9 slice.29
  241.8 0.0 copy-start.6
  241.8 0.7 slice_bitcast_fusion
  242.5 0.6 copy.50
  243.1 1.3 slice_reduce_fusion
  244.4 0.2 slice.28
  244.6 2.2 copy.47
  246.8 0.0 copy-done.1
  246.8 0.6 convert_bitcast_fusion
  247.4 4.7 %copy.35 = f32[2,256,4,512]{3,2,1,0:T(4,128)} copy(f32[2,256,4,512]{3,1,2,0:T(8,128)S(1)} %convert_bitcast_fusion) | data formatting | bytes 8388608
  252.1 0.1 convert_bitcast_fusion.1
  252.3 1.9 copy.36
  254.1 0.0 copy-done.6
  254.1 0.6 copy.52
  (17 shorter events, 0.1 us)
Async XLA Ops:
  0.6 3.4 %copy-start.2 = (bf16[2,100,4,512]{3,2,1,0:T(4,128)(2,1)S(1)}, bf16[2,100,4,512]{3,2,1,0:T(4,128)(2,1)}, u32[]{:S(2)}) copy-start(bf16[2,100,4,512]{3,2,1,0:T(4,128)(2,1)} %param.16) | copy-start | bytes 2457604
  4.0 1.2 copy-start.3
  4.2 2.8 %copy-start.5 = (bf16[2,275,100]{2,0,1:T(2,128)(2,1)S(1)}, bf16[2,275,100]{2,0,1:T(2,128)(2,1)}, u32[]{:S(2)}) copy-start(bf16[2,275,100]{2,0,1:T(2,128)(2,1)} %param.15) | copy-start | bytes 330004
  5.3 2.5 copy-start.7
  5.3 3.1 %copy-start.8 = (bf16[2,4,512]{2,1,0:T(4,128)(2,1)S(1)}, bf16[2,4,512]{2,1,0:T(4,128)(2,1)}, u32[]{:S(2)}) copy-start(bf16[2,4,512]{2,1,0:T(4,128)(2,1)} %param.19) | copy-start | bytes 24580
  5.3 3.1 %copy-start.9 = (bf16[2,4,512]{2,1,0:T(4,128)(2,1)S(1)}, bf16[2,4,512]{2,1,0:T(4,128)(2,1)}, u32[]{:S(2)}) copy-start(bf16[2,4,512]{2,1,0:T(4,128)(2,1)} %param.18) | copy-start | bytes 24580
  5.3 3.7 %copy-start.10 = (bf16[2,275]{1,0:T(2,128)(2,1)S(1)}, bf16[2,275]{1,0:T(2,128)(2,1)}, u32[]{:S(2)}) copy-start(bf16[2,275]{1,0:T(2,128)(2,1)} %param.21) | copy-start | bytes 3304
  239.0 5.4 %copy-start = (bf16[2,448,512]{2,1,0:T(8,128)(2,1)S(1)}, bf16[2,448,512]{2,1,0:T(8,128)(2,1)}, u32[]{:S(2)}) copy-start(bf16[2,448,512]{2,1,0:T(8,128)(2,1)} %get-tuple-element.13) | copy-start | bytes 2752516
  241.8 12.4 %copy-start.6 = (f32[2,4,1,512]{3,1,0,2:T(4,128)}, f32[2,4,1,512]{3,1,0,2:T(4,128)S(1)}, u32[]{:S(2)}) copy-start(f32[2,4,1,512]{3,1,0,2:T(4,128)S(1)} %copy.49) | copy-start | bytes 49156
  244.6 2.2 copy-start.1
  247.4 4.7 %copy-start.4 = (bf16[2,288,512]{2,1,0:T(8,128)(2,1)S(1)}, bf16[2,288,512]{2,1,0:T(8,128)(2,1)}, u32[]{:S(2)}) copy-start(bf16[2,288,512]{2,1,0:T(8,128)(2,1)} %get-tuple-element.15) | copy-start | bytes 1769476

commit v4 on v3

--- a/solution.py
+++ b/solution.py
@@ -125,9 +125,9 @@
 
 def kernel(
     dims,
-    chars_ref, targets_ref, lang_ref, bias_ref, win_in, wrec_in, wdec_in, emb_ref, bdec_ref, mask_ref,
+    chars_ref, targets_ref, lang_ref, b_in_ref, b_rec_ref, win_in, wrec_in, wdec_in, emb_ref, b_dec_ref, masks_ref,
     grec_out, gwin_out, gwd_out, small_out,
-    idsrc, idsall, idtmp, ids, bias, win, W, wd, x, xp, allowed, acc, st, stp, gs, cell, lg, lgp, lossv, gb,
+    idsrc, idsall, idtmp, ids, bdec, masks, bias, win, W, wd, x, xp, allowed, acc, st, stp, gs, cell, lg, lgp, lossv, gb,
     dh, cg, pg, pgx, psend, precv, dW, gwin, gemb, gwd, gwd_s, gwd_r, gwd_all, gwin_s, gwin_r, gwin_all,
     recvB, epart, esend, erecv, eall,
     lsem, ids_s, ids_r, win_s2, win_r2, bias_s, bias_r, wdy_s, wdy_r, wdc_s, wdc_r, wz_s, wz_r, wx_s, wx_r, wc_s, wc_r,
@@ -209,7 +209,7 @@
     def wz_copy(j, n):
         columns = pl.ds(pl.multiple_of(flip(g, Z_STEPS[j][1]) * U, U), U)
         there = wrec_in.at[flip(d, Z_STEPS[j][0]), gates_of(n), rows_in(n), columns]
-        return copy_to(there, W.at[c, gates_of(n), rows_of(d, g, r, n), :], wz_s.at[j, n], wz_r.at[j, n], z_dev(j))
+        return copy_to(there, W.at[c, gates_of(n), rows_of(d, g, r, n), :], wz_s.at[j], wz_r.at[j, n], z_dev(j))
 
     def z_block(j):
         steps = Z_STEPS[j] if j < 3 else (0, 0)
@@ -221,11 +221,14 @@
 
     def wx_copy(j, k, n):
         block = w_block(c, j, 0, n)
-        return copy_to(block, block, wx_s.at[j, k - 1, n], wx_r.at[j, k - 1, n], r_dev(k))
-
-    def wc_copy(j, k, n, core):
-        block = w_block(core, j, k, n)
-        return copy_to(block, block, wc_s.at[j, k, n], wc_r.at[j, k, n], partner)
+        return copy_to(block, block, wx_s.at[k - 1], wx_r.at[j, k - 1, n], r_dev(k))
+
+    def wc_copy(j, k, n):
+        block = w_block(c, j, k, n)
+        return copy_to(block, block, wc_s.at[0], wc_r.at[0], partner)
+
+    def wc_all(core):
+        return copy_to(W.at[core], W.at[core], wc_s.at[0], wc_r.at[0], partner)
 
     def wd_rows(yy):
         return wd.at[pl.ds(yy * 2, 2), c]
@@ -263,7 +266,7 @@
         idsrc[dd, 2 * P8 : 2 * P8 + 8, 0:RL] = jnp.broadcast_to(lang_ref[...].astype(F32), (8, RL))
     for j in range(3):
         ids_copy(j).start()
-    bias[c, 0:4] = bias_ref[d, :, half]
+    bias[c, 0:4] = b_in_ref[d, :, half].astype(F32) + b_rec_ref[d, :, half].astype(F32)
     bias_copy.start()
     idsall[part] = idsrc[d]
 
@@ -271,7 +274,7 @@
     for n in range(pieces):
         for k in range(1, RR):
             wx_copy(3, k, n).start()
-        wc_copy(3, 0, n, c).start()
+        wc_copy(3, 0, n).start()
 
     dW[...] = jnp.zeros_like(dW)
     gwin[...] = jnp.zeros_like(gwin)
@@ -280,6 +283,10 @@
     gb[...] = jnp.zeros_like(gb)
     cg[...] = jnp.zeros_like(cg)
     cell[0] = jnp.zeros_like(cell[0])
+    bdec[...] = jnp.zeros_like(bdec)
+    bdec[0:2, 0 : dims.V] = b_dec_ref[...].astype(F32)
+    masks[...] = jnp.zeros_like(masks)
+    masks[0 : dims.LANGS, 0 : dims.V] = masks_ref[...].astype(F32)
     idtmp[...] = jnp.zeros_like(idtmp)
 
     for j in range(3):
@@ -301,9 +308,9 @@
     def char_hot(t):
         return jnp.where(vocab == id_column(place(t)), 1.0, 0.0).astype(BF16)
 
-    lang_lane = lax.broadcasted_iota(jnp.int32, (NR, mask_ref.shape[0]), 1).astype(F32)
+    lang_lane = lax.broadcasted_iota(jnp.int32, (NR, masks.shape[0]), 1).astype(F32)
     lang_hot = jnp.where(lang_lane == id_column(2 * P8), 1.0, 0.0).astype(BF16)
-    allowed[...] = dot(lang_hot, mask_ref[...])
+    allowed[...] = dot(lang_hot, masks[...].astype(BF16))
 
     @pl.loop(0, L)
     def _(t):
@@ -366,16 +373,14 @@
             wz_copy(j, n).wait_recv()
             for k in range(1, RR):
                 wx_copy(j, k, n).start()
-            wc_copy(j, 0, n, c).start()
+            wc_copy(j, 0, n).start()
             if n + WINDOW < pieces:
                 wz_copy(j, n + WINDOW).start()
         j, n = from_x[at]
         for k in range(1, RR):
             wx_copy(j, k, n).wait_recv()
-            wc_copy(j, k, n, c).start()
-    for j, n in from_x:
-        for k in range(RR):
-            wc_copy(j, k, n, 1 - c).wait_recv()
+            wc_copy(j, k, n).start()
+    wc_all(1 - c).wait_recv()
     for k in range(Hy):
         yy = lax.rem(y + Hy - k, Hy)
         other = wd.at[pl.ds(yy * 2, 2), 1 - c]
@@ -389,7 +394,7 @@
 
     def decode(t):
         stp_copy(t).start()
-        logits = bdec_ref[d]
+        logits = bdec[pl.ds(d, 1), :]
         for m in range(2 * Hy):
             logits = logits + dot(st[t, m], wd[m].reshape(U2, VP))
         masked = jnp.where(allowed[...] > 0.5, logits, masked_value)
@@ -425,13 +430,13 @@
                 f_copy(t, b, p).start()
         decode(t - 1)
 
-    for j, n in from_x:
-        if j < 3:
-            wz_copy(j, n).wait_send()
-        for k in range(1, RR):
-            wx_copy(j, k, n).wait_send()
-        for k in range(RR):
-            wc_copy(j, k, n, c).wait_send()
+    block = wrec_in.at[d, :, :, half]
+    for j in range(3):
+        copy_to(block, block, wz_s.at[j], wz_r.at[j, 0], z_dev(j)).wait_send()
+    blocks = W.at[c, :, 0 : 4 * KR, :]
+    for k in range(1, RR):
+        copy_to(blocks, blocks, wx_s.at[k - 1], wx_r.at[0, k - 1, 0], r_dev(k)).wait_send()
+    wc_all(c).wait_send()
 
     @pl.loop(0, dims.H // U)
     def _(k):
@@ -673,16 +678,16 @@
     def b_out(i, k, n):
         return copy_to(
             W.at[0, gates_of(n), out_rows(i, k, n), :], recvB.at[k - 1, i, gates_of(n), rows_in(n), :],
-            B_s.at[k - 1, i, n], B_r.at[k - 1, i, n], r_dev(k),
+            B_s.at[k - 1], B_r.at[k - 1, i, n], r_dev(k),
         )
 
     def c_out(i, n):
         there = grec_out.at[d, gates_of(n), rows_in(n), half]
-        return copy_to(W.at[1, gates_of(n), out_rows(i, 0, n), :], there, C_s.at[i, n], C_r.at[i, n], z_dev(i))
+        return copy_to(W.at[1, gates_of(n), out_rows(i, 0, n), :], there, C_s.at[i], C_r.at[i], z_dev(i))
 
     def own_out(n):
         there = grec_out.at[d, gates_of(n), rows_in(n), half]
-        return pltpu.make_async_copy(W.at[1, gates_of(n), out_rows(3, 0, n), :], there, C_s.at[3, n])
+        return pltpu.make_async_copy(W.at[1, gates_of(n), out_rows(3, 0, n), :], there, C_s.at[3])
 
     def gates_in(n):
         return range(n // KP * QN, (n // KP + 1) * QN)
@@ -853,13 +858,12 @@
     e_core.wait_send()
     dec_sum.drain()
     in_sum.drain()
-    for i, n in steps:
-        for k in range(1, RR):
-            b_out(i, k, n).wait_send()
-        if i < 3:
-            c_out(i, n).wait()
-        else:
-            own_out(n).wait()
+    for k in range(1, RR):
+        copy_to(W.at[0, :, 0 : 4 * KR, :], W.at[0, :, 0 : 4 * KR, :], B_s.at[k - 1], B_r.at[k - 1, 0, 0], r_dev(k)).wait_send()
+    kept = grec_out.at[d, :, :, half]
+    for i in range(3):
+        copy_to(kept, kept, C_s.at[i], C_r.at[i], z_dev(i)).wait()
+    pltpu.make_async_copy(kept, kept, C_s.at[3]).wait()
     own_small.wait()
 
 
@@ -879,6 +883,8 @@
         vmem((4, id_rows, 128), F32),
         vmem((128, 128), F32),
         vmem((4, dims.RL // 2, 128), F32),
+        vmem((8, VP), F32),
+        vmem((ceil_to(dims.LANGS, 16), VP), F32),
         vmem((2, 8, U), F32),
         vmem((2, 4, EP, U), BF16),
         vmem((2, 4, H, U), BF16),
@@ -922,9 +928,9 @@
         sem((1,)), sem((1,)),
         sem((along,)), sem((along,)),
         sem((Hy,)), sem((Hy,)),
-        sem((3, pieces)), sem((3, pieces)),
-        sem((4, groups, pieces)), sem((4, groups, pieces)),
-        sem((4, RR, pieces)), sem((4, RR, pieces)),
+        sem((3,)), sem((3, pieces)),
+        sem((groups,)), sem((4, groups, pieces)),
+        sem((1,)), sem((1,)),
         sem((1,)), sem((1,)),
         sem((2, BATCHES, peers)), sem((2, BATCHES, peers)),
         sem((L,)), sem((L,)),
@@ -933,8 +939,8 @@
         sem((L,)), sem((L,)),
         sem((2, 2 * groups + 3)),
         sem((2, 2 * groups + 3)),
-        sem((groups, 4, pieces)), sem((groups, 4, pieces)),
-        sem((4, pieces)), sem((4, pieces)),
+        sem((groups,)), sem((groups, 4, pieces)),
+        sem((4,)), sem((3,)),
         sem((stages + 2,)), sem((stages + 2,)),
     ]
     rows = NR * L
@@ -947,7 +953,7 @@
             jax.ShapeDtypeStruct((2, N_DEC, 2 * U), BF16),
             jax.ShapeDtypeStruct((2, VS, 128), F32),
         ),
-        in_specs=[inside] * 4 + [apart] * 3 + [inside] * 3,
+        in_specs=[inside] * 5 + [apart] * 3 + [inside] * 3,
         out_specs=(apart, apart, apart, apart),
         scratch_shapes=scratch,
         cost_estimate=pl.CostEstimate(flops=flops, bytes_accessed=8 << 20, transcendentals=rows * U2 * 8),
@@ -956,6 +962,55 @@
         ),
         name="train_step",
     )(*operands)
+
+
+def outputs_kernel(
+    dims, grec, gwin, gwd, small, w_rec_out, w_in_out, b_in_out, b_rec_out, w_dec_out, emb_out, b_dec_out, loss_out
+):
+    for d in range(2):
+        for q in range(4):
+            w_rec_out[d, :, q, :] = grec[d, q].astype(F32)
+
+    @pl.when(pl.program_id(0) == 0)
+    def _():
+        E, EW, V, V8 = dims.E, dims.EW, dims.V, dims.V8
+        for d in range(2):
+            for q in range(4):
+                w_in_out[d, :, q, :] = gwin[d, q * EW : q * EW + E].astype(F32)
+                first = q * EW + E // 16 * 16
+                row = gwin[d, first : first + 16].astype(F32)[E % 16 : E % 16 + 1]
+                b_in_out[d, q : q + 1, :] = row
+                b_rec_out[d, q : q + 1, :] = row
+            w_dec_out[:, d, :] = gwd[d, 0:V].astype(F32)
+            emb_out[:, d, :] = small[d, 0:V, 0:E]
+            for k in range(dims.VP // 128):
+                width = min(128, V - k * 128)
+                b_dec_out[d : d + 1, k * 128 : k * 128 + width] = small[d, V8 + k : V8 + k + 1, 0:width]
+        at = V8 + dims.VP // 128
+        loss_out[...] = small[0, at : at + 1, 0:1] + small[1, at : at + 1, 0:1]
+
+
+def call_outputs(dims, grec, gwin, gwd, small):
+    KR, U2, E, V = dims.KR, dims.U2, dims.E, dims.V
+    parts = 4 if KR % 64 == 0 else 1
+    rows = KR // parts
+
+    def whole(*shape):
+        return pl.BlockSpec(shape, lambda i: (0,) * len(shape))
+
+    shapes = ((2, E, 4, U2), (2, 4, U2), (2, 4, U2), (V, 2, U2), (V, 2, E), (2, V), (1, 1))
+    return pl.pallas_call(
+        functools.partial(outputs_kernel, dims),
+        grid=(parts,),
+        out_shape=[jax.ShapeDtypeStruct((2, KR, 4, U2), F32)] + [jax.ShapeDtypeStruct(s, F32) for s in shapes],
+        in_specs=[
+            pl.BlockSpec((2, 4, rows, U2), lambda i: (0, 0, i, 0)),
+            whole(*gwin.shape), whole(*gwd.shape), whole(*small.shape),
+        ],
+        out_specs=[pl.BlockSpec((2, rows, 4, U2), lambda i: (0, i, 0, 0))] + [whole(*s) for s in shapes],
+        compiler_params=pltpu.CompilerParams(vmem_limit_bytes=62 << 20),
+        name="outputs",
+    )(grec, gwin, gwd, small)
 
 
 def local(
@@ -973,38 +1028,26 @@
     )
     VP, EP, EW = dims.VP, dims.EP, dims.EW
 
-    bias = b_in.astype(F32) + b_rec.astype(F32)
     win = jnp.pad(w_in.transpose(0, 2, 1, 3), ((0, 0), (0, 0), (0, EP - E), (0, 0)))
     wrec = w_rec.transpose(0, 2, 1, 3)
     wdec = jnp.pad(w_dec, ((0, 0), (0, 0), (0, VP - V))).reshape(2, 2, U, VP)
     emb = jnp.concatenate([embedding, jnp.ones((2, V, 1), BF16)], axis=2)
     emb = jnp.pad(emb, ((0, 0), (0, VP - V), (0, EP - E - 1)))
-    bdec = jnp.pad(b_dec.astype(F32), ((0, 0), (0, VP - V)))[:, None, :]
-    lang_rows = ceil_to(dims.LANGS, 16)
-    mask = jnp.pad(vocab_masks.astype(BF16), ((0, lang_rows - dims.LANGS), (0, VP - V)))
-
-    grec, gwin, gwd, small = call_kernel(
-        dims, char_ids.T, targets.transpose(0, 2, 1), lang_ids[None], bias, win, wrec, wdec, emb, bdec, mask
+
+    sums = call_kernel(
+        dims, char_ids.T, targets.transpose(0, 2, 1), lang_ids[None], b_in, b_rec, win, wrec, wdec, emb, b_dec,
+        vocab_masks,
     )
-
-    grad_w_rec = grec.astype(F32).transpose(0, 2, 1, 3)
-    gwin = gwin[:, : 4 * EW].reshape(2, 4, EW, units).astype(F32)
-    grad_w_in = gwin[:, :, :E].transpose(0, 2, 1, 3)
-    grad_bias = gwin[:, :, E]
-    grad_w_dec = gwd[:, :V].astype(F32).transpose(0, 2, 1)
-    V8 = dims.V8
-    grad_embedding = small[:, :V, :E]
-    grad_b_dec = small[:, V8 : V8 + VP // 128].reshape(2, VP)[:, :V]
-    total_loss = jnp.sum(small[:, V8 + VP // 128, 0])
+    w_rec_grad, w_in_grad, b_in_grad, b_rec_grad, w_dec_grad, emb_grad, b_dec_grad, loss = call_outputs(dims, *sums)
     return (
-        total_loss,
-        grad_embedding,
-        grad_w_in,
-        grad_w_rec,
-        grad_bias,
-        grad_bias,
-        grad_w_dec,
-        grad_b_dec,
+        loss[0, 0],
+        emb_grad.transpose(1, 0, 2),
+        w_in_grad,
+        w_rec_grad,
+        b_in_grad,
+        b_rec_grad,
+        w_dec_grad.transpose(1, 2, 0),
+        b_dec_grad,
     )
 
 

time: 255 us -> 243 us (0.953)
  local copies, waits for them, and re-layouts: 21.3 us -> 7.16 us
  Pallas kernels: 229 us -> 234 us
  other arithmetic: 3.34 us -> 0.72 us
    unnamed x34 -> x8, local copies, waits for them, and re-layouts: 15.9 us -> 5.13 us
    pallas_call x0 -> x1, Pallas kernels: none -> 6.78 us  [call_outputs(): pl.pallas_call(functools.partial(outputs_kernel, dims), grid=(parts,), ou...]
where the time goes in v4:
time: 243 us
  Pallas kernels  234 us (96%)
  local copies, waits for them, and re-layouts  7.16 us (3%)
    pallas_call x1, Pallas kernels, call_kernel(): pl.pallas_call(functools.partial(kernel, dims), out_shape=(jax.ShapeDtype...  228 us
    pallas_call x1, Pallas kernels, call_outputs(): pl.pallas_call(functools.partial(outputs_kernel, dims), grid=(parts,), ou...  6.78 us
    unnamed x8, local copies, waits for them, and re-layouts  5.13 us

profile of v4, /device:TPU:0, one launch (start us, length us, event | category | flops | bytes accessed | tf_op | source)
XLA Modules:
  0.0 243.1 jit_solution(8945124608672543122)
XLA Ops:
  0.6 0.0 copy-start.1
  0.6 1.0 copy.22
  1.6 0.7 fusion.2.emb_ref
  2.4 1.5 copy.23
  3.9 1.0 pad.14.clone
  4.8 0.0 copy-start
  4.8 0.0 copy-done.1
  4.8 0.2 copy.27
  5.0 1.1 pad.13.win_in
  6.1 0.7 copy-done
  6.8 1.7 copy.26
  8.5 227.7 %train_step.1 = (bf16[2,4,256,512]{3,2,1,0:T(8,128)(2,1)}, bf16[2,448,512]{2,1,0:T(8,128)(2,1)}, bf16[2,288,512]{2,1,0:T(8,128)(2,1)}, f32[2,288,128]{2,1,0:T(8,128)}) custom-call(s32[8,64]{1,0:T(8,128)} %bitcast.19, s32[2,8,64]{2,1,0:T(8,128)} %bitcast.18, s32[1,64]{1,0:T(1,128)} %bitcast.20, bf16[2,4,512]{2,1,0:T(4,128)(2,1)} %b_in_ref.1, ...), custom_call_target="tpu_custom_call" | custom-call | flops 30601641984 | bytes 8388608 | tf_op jit(solution)/shard_map/train_step/pallas_call | solution.py:948
  236.2 6.8 %outputs.1 = (f32[2,256,4,512]{3,2,1,0:T(4,128)}, f32[2,100,4,512]{3,2,1,0:T(4,128)}, f32[2,4,512]{2,1,0:T(4,128)}, f32[2,4,512]{2,1,0:T(4,128)}, f32[275,2,512]...) custom-call(bf16[2,4,256,512]{3,2,1,0:T(8,128)(2,1)} %get-tuple-element.20.grec, ...), custom_call_target="tpu_custom_call" | custom-call | tf_op jit(solution)/shard_map/outputs/pallas_call | solution.py:1002
Async XLA Ops:
  0.6 4.2 %copy-start.1 = (bf16[2,100,4,512]{3,2,1,0:T(4,128)(2,1)S(1)}, bf16[2,100,4,512]{3,2,1,0:T(4,128)(2,1)}, u32[]{:S(2)}) copy-start(bf16[2,100,4,512]{3,2,1,0:T(4,128)(2,1)} %param.16) | copy-start | bytes 2457604
  4.8 2.0 copy-start

commit v5 on v4

--- a/solution.py
+++ b/solution.py
@@ -15,7 +15,7 @@
 ROW_PARTS = 2
 AHEAD = 8
 EARLY = 2
-WINDOW = 2
+WINDOW = 3
 BATCHES = 2
 
 
@@ -336,10 +336,10 @@
     def gates(t, b):
         rows = part_rows(b)
         for cc in range(2):
-            si = jax.nn.sigmoid(acc[cc, 0])
-            sf = jax.nn.sigmoid(acc[cc, 1])
-            tg = jnp.tanh(acc[cc, 2])
-            so = jax.nn.sigmoid(acc[cc, 3])
+            si = jax.nn.sigmoid(acc[cc, 0, rows])
+            sf = jax.nn.sigmoid(acc[cc, 1, rows])
+            tg = jnp.tanh(acc[cc, 2, rows])
+            so = jax.nn.sigmoid(acc[cc, 3, rows])
             new = sf * cell[t, cc, rows] + si * tg
             cell[t + 1, cc, rows] = new
             st[t, mine, rows, cc * U : (cc + 1) * U] = (so * jnp.tanh(new)).astype(BF16)
@@ -352,10 +352,10 @@
         yy = lax.rem(y + Hy - peers[p][1], Hy)
         return yy * 2 + flip(g, peers[p][0])
 
+    for cc in range(2):
+        for q in range(4):
+            acc[cc, q] = dot(x[0], win[cc, q]) + bias[cc, q : q + 1]
     for b in range(BATCHES):
-        for cc in range(2):
-            for q in range(4):
-                acc[cc, q] = dot(x[0, part_rows(b)], win[cc, q]) + bias[cc, q : q + 1]
         gates(0, b)
         for p in range(len(peers)):
             f_copy(0, b, p).start()
@@ -411,18 +411,18 @@
 
     @pl.loop(1, L)
     def _(t):
+        for cc in range(2):
+            for q in range(4):
+                start = dot(x[t], win[cc, q]) + bias[cc, q : q + 1]
+                acc[cc, q] = start + dot(st[t - 1, mine], W[cc, q, chip_rows(mine), :])
         for b in range(BATCHES):
             rows = part_rows(b)
-            for cc in range(2):
-                for q in range(4):
-                    start = dot(x[t, rows], win[cc, q]) + bias[cc, q : q + 1]
-                    acc[cc, q] = start + dot(st[t - 1, mine, rows], W[cc, q, chip_rows(mine), :])
             for p in reversed(range(len(peers))):
                 f_copy(t - 1, b, p).wait_recv()
                 m = peer_block(p)
                 for cc in range(2):
                     for q in range(4):
-                        acc[cc, q] += dot(st[t - 1, m, rows], W[cc, q, chip_rows(m), :])
+                        acc[cc, q, rows] += dot(st[t - 1, m, rows], W[cc, q, chip_rows(m), :])
             gates(t, b)
             for p in range(len(peers)):
                 f_copy(t - 1, b, p).wait_send()
@@ -477,13 +477,13 @@
             pg[slot, cc, 3, rows] = (h * tc * so * (1.0 - so)).astype(BF16)
             cg[cc, rows] = total * sf
 
-    def partial(t, b, m, cc):
+    def partial(t, rows_here, m, cc):
         slot = lax.rem(t, 2)
         rows = pl.ds(pl.multiple_of(m * U2 + cc * U, U), U)
         total = None
         for kk in range(2):
             for q in range(4):
-                term = dot(pg[slot, kk, q, part_rows(b)], W[kk, q, rows, :])
+                term = dot(pg[slot, kk, q, rows_here], W[kk, q, rows, :])
                 total = term if total is None else total + term
         return total
 
@@ -601,13 +601,6 @@
     for cc in range(2):
         dh[cc] = dec_back(L - 1, cc)
 
-    @pl.loop(0, L)
-    def _(t):
-        stp_copy(t).wait()
-        lgp_copy(t).wait()
-
-    xp_copy.wait()
-
     @pl.loop(0, L - 1)
     def _(i):
         t = L - 1 - i
@@ -633,22 +626,30 @@
             for p in range(len(peers)):
                 m = add_y(peers[p][1]) * 2 + flip(g, peers[p][0])
                 for cc in range(2):
-                    psend[slot, p, rows, cc * U : (cc + 1) * U] = partial(t, b, m, cc).astype(BF16)
+                    psend[slot, p, rows, cc * U : (cc + 1) * U] = partial(t, rows, m, cc).astype(BF16)
                 b_copy(t, b, p).start()
-            for cc in range(2):
-                dh[cc, rows] = partial(t, b, mine, cc)
         pgx_copy(t).start()
         for cc in range(2):
-            dh[cc] += dec_back(t - 1, cc)
+            dh[cc] = partial(t, pl.ds(0, NR), mine, cc) + dec_back(t - 1, cc)
 
         @pl.when(i > 0)
         def _():
             pgx_copy(t + 1).wait_recv()
             rec_grads(t + 1)
+
+        @pl.when((i > 0) & (i < L - 2))
+        def _():
             in_grads(t + 1)
 
         @pl.when(i == 0)
         def _():
+            xp_copy.wait()
+
+            @pl.loop(0, L)
+            def _(at):
+                stp_copy(at).wait()
+                lgp_copy(at).wait()
+
             decoder_grad()
 
         @pl.when(i == 1)
@@ -734,6 +735,7 @@
     ahead = min(AHEAD, len(steps))
     for at in range(ahead):
         send_over(at)
+    in_grads(2)
     in_grads(1)
 
     pgx_copy(2).wait_send()
@@ -892,7 +894,7 @@
         vmem((L, NR, EP), BF16),
         vmem((L, NR, EP), BF16),
         vmem((NR, VP), F32),
-        vmem((2, 4, RB, U), F32),
+        vmem((2, 4, NR, U), F32),
         vmem((L, chips, NR, U2), BF16),
         vmem((L, chips, NR, U2), BF16),
         vmem((L, 4, 2, NR, U), F32),
@@ -971,9 +973,11 @@
         for q in range(4):
             w_rec_out[d, :, q, :] = grec[d, q].astype(F32)
 
+    E, EW, V, V8 = dims.E, dims.EW, dims.V, dims.V8
+    steps = pl.num_programs(0)
+
     @pl.when(pl.program_id(0) == 0)
     def _():
-        E, EW, V, V8 = dims.E, dims.EW, dims.V, dims.V8
         for d in range(2):
             for q in range(4):
                 w_in_out[d, :, q, :] = gwin[d, q * EW : q * EW + E].astype(F32)
@@ -981,7 +985,15 @@
                 row = gwin[d, first : first + 16].astype(F32)[E % 16 : E % 16 + 1]
                 b_in_out[d, q : q + 1, :] = row
                 b_rec_out[d, q : q + 1, :] = row
+
+    @pl.when(pl.program_id(0) == steps // 4)
+    def _():
+        for d in range(2):
             w_dec_out[:, d, :] = gwd[d, 0:V].astype(F32)
+
+    @pl.when(pl.program_id(0) == steps // 2)
+    def _():
+        for d in range(2):
             emb_out[:, d, :] = small[d, 0:V, 0:E]
             for k in range(dims.VP // 128):
                 width = min(128, V - k * 128)

time: 243 us -> 239 us (0.984)
  Pallas kernels: 234 us -> 230 us
    pallas_call x1, Pallas kernels: 228 us -> 223 us  [call_kernel(): pl.pallas_call(functools.partial(kernel, dims), out_shape=(jax.ShapeDtype...]
where the time goes in v5:
time: 239 us
  Pallas kernels  230 us (96%)
  local copies, waits for them, and re-layouts  7.16 us (3%)
    pallas_call x1, Pallas kernels, call_kernel(): pl.pallas_call(functools.partial(kernel, dims), out_shape=(jax.ShapeDtype...  223 us
    pallas_call x1, Pallas kernels, call_outputs(): pl.pallas_call(functools.partial(outputs_kernel, dims), grid=(parts,), ou...  6.43 us
    unnamed x8, local copies, waits for them, and re-layouts  5.13 us

profile of v5, /device:TPU:0, one launch (start us, length us, event | category | flops | bytes accessed | tf_op | source)
XLA Modules:
  0.0 238.6 jit_solution(1235343921249334574)
XLA Ops:
  0.6 0.0 copy-start.1
  0.6 1.0 copy.22
  1.6 0.7 fusion.2.emb_ref
  2.4 1.5 copy.23
  3.9 1.0 pad.14.clone
  4.8 0.0 copy-start
  4.8 0.0 copy-done.1
  4.8 0.2 copy.27
  5.0 1.1 pad.13.win_in
  6.1 0.7 copy-done
  6.8 1.7 copy.26
  8.5 223.4 %train_step.1 = (bf16[2,4,256,512]{3,2,1,0:T(8,128)(2,1)}, bf16[2,448,512]{2,1,0:T(8,128)(2,1)}, bf16[2,288,512]{2,1,0:T(8,128)(2,1)}, f32[2,288,128]{2,1,0:T(8,128)}) custom-call(s32[8,64]{1,0:T(8,128)} %bitcast.19, s32[2,8,64]{2,1,0:T(8,128)} %bitcast.18, s32[1,64]{1,0:T(1,128)} %bitcast.20, bf16[2,4,512]{2,1,0:T(4,128)(2,1)} %b_in_ref.1, ...), custom_call_target="tpu_custom_call" | custom-call | flops 30601641984 | bytes 8388608 | tf_op jit(solution)/shard_map/train_step/pallas_call | solution.py:950
  232.0 6.4 %outputs.1 = (f32[2,256,4,512]{3,2,1,0:T(4,128)}, f32[2,100,4,512]{3,2,1,0:T(4,128)}, f32[2,4,512]{2,1,0:T(4,128)}, f32[2,4,512]{2,1,0:T(4,128)}, f32[275,2,512]...) custom-call(bf16[2,4,256,512]{3,2,1,0:T(8,128)(2,1)} %get-tuple-element.20.grec, ...), custom_call_target="tpu_custom_call" | custom-call | tf_op jit(solution)/shard_map/outputs/pallas_call | solution.py:1014
Async XLA Ops:
  0.6 4.2 %copy-start.1 = (bf16[2,100,4,512]{3,2,1,0:T(4,128)(2,1)S(1)}, bf16[2,100,4,512]{3,2,1,0:T(4,128)(2,1)}, u32[]{:S(2)}) copy-start(bf16[2,100,4,512]{3,2,1,0:T(4,128)(2,1)} %param.16) | copy-start | bytes 2457604
  4.8 2.0 copy-start

commit v6 on v5

--- a/solution.py
+++ b/solution.py
@@ -426,7 +426,7 @@
             gates(t, b)
             for p in range(len(peers)):
                 f_copy(t - 1, b, p).wait_send()
-            for p in range(len(peers)):
+            for p in reversed(range(len(peers))):
                 f_copy(t, b, p).start()
         decode(t - 1)
 
@@ -821,14 +821,14 @@
 
     e_start(0)
     between = [
-        (0.05, lambda: e_take(0)),
-        (0.2, lambda: in_sum.add(in_share())),
-        (0.2, lambda: e_take(1)),
-        (0.35, lambda: e_take(2)),
-        (0.5, in_sum.relay),
-        (0.6, e_gather),
-        (0.7, in_sum.spread),
-        (0.8, e_finish),
+        (0.1, lambda: e_take(0)),
+        (0.3, lambda: in_sum.add(in_share())),
+        (0.3, lambda: e_take(1)),
+        (0.5, lambda: e_take(2)),
+        (0.6, in_sum.relay),
+        (0.8, e_gather),
+        (0.85, in_sum.spread),
+        (0.9, e_finish),
         (1.0, in_sum.finish),
     ]
     for at in range(sent, len(steps)):

time: 239 us -> 238 us (level)
  no operation moved by 1% of the time
where the time goes in v6:
time: 238 us
  Pallas kernels  229 us (96%)
  local copies, waits for them, and re-layouts  7.16 us (3%)
    pallas_call x1, Pallas kernels, call_kernel(): pl.pallas_call(functools.partial(kernel, dims), out_shape=(jax.ShapeDtype...  222 us
    pallas_call x1, Pallas kernels, call_outputs(): pl.pallas_call(functools.partial(outputs_kernel, dims), grid=(parts,), ou...  6.43 us
    unnamed x8, local copies, waits for them, and re-layouts  5.13 us

profile of v6, /device:TPU:0, one launch (start us, length us, event | category | flops | bytes accessed | tf_op | source)
XLA Modules:
  0.0 237.6 jit_solution(2671156930643887316)
XLA Ops:
  0.6 0.0 copy-start.1
  0.6 1.0 copy.22
  1.6 0.7 fusion.2.emb_ref
  2.4 1.5 copy.23
  3.9 1.0 pad.14.clone
  4.8 0.0 copy-start
  4.8 0.0 copy-done.1
  4.8 0.2 copy.27
  5.0 1.1 pad.13.win_in
  6.1 0.7 copy-done
  6.8 1.7 copy.26
  8.5 222.4 %train_step.1 = (bf16[2,4,256,512]{3,2,1,0:T(8,128)(2,1)}, bf16[2,448,512]{2,1,0:T(8,128)(2,1)}, bf16[2,288,512]{2,1,0:T(8,128)(2,1)}, f32[2,288,128]{2,1,0:T(8,128)}) custom-call(s32[8,64]{1,0:T(8,128)} %bitcast.19, s32[2,8,64]{2,1,0:T(8,128)} %bitcast.18, s32[1,64]{1,0:T(1,128)} %bitcast.20, bf16[2,4,512]{2,1,0:T(4,128)(2,1)} %b_in_ref.1, ...), custom_call_target="tpu_custom_call" | custom-call | flops 30601641984 | bytes 8388608 | tf_op jit(solution)/shard_map/train_step/pallas_call | solution.py:950
  231.0 6.4 %outputs.1 = (f32[2,256,4,512]{3,2,1,0:T(4,128)}, f32[2,100,4,512]{3,2,1,0:T(4,128)}, f32[2,4,512]{2,1,0:T(4,128)}, f32[2,4,512]{2,1,0:T(4,128)}, f32[275,2,512]...) custom-call(bf16[2,4,256,512]{3,2,1,0:T(8,128)(2,1)} %get-tuple-element.20.grec, ...), custom_call_target="tpu_custom_call" | custom-call | tf_op jit(solution)/shard_map/outputs/pallas_call | solution.py:1014
Async XLA Ops:
  0.6 4.2 %copy-start.1 = (bf16[2,100,4,512]{3,2,1,0:T(4,128)(2,1)S(1)}, bf16[2,100,4,512]{3,2,1,0:T(4,128)(2,1)}, u32[]{:S(2)}) copy-start(bf16[2,100,4,512]{3,2,1,0:T(4,128)(2,1)} %param.16) | copy-start | bytes 2457604
  4.8 2.0 copy-start

commit v7 on v6

--- a/solution.py
+++ b/solution.py
@@ -967,7 +967,8 @@
 
 
 def outputs_kernel(
-    dims, grec, gwin, gwd, small, w_rec_out, w_in_out, b_in_out, b_rec_out, w_dec_out, emb_out, b_dec_out, loss_out
+    dims, grec, gwin, gwd, small, w_rec_out, w_in_out, b_in_out, b_rec_out, w_dec_out, emb_out, b_dec_out, loss_out,
+    w_in_all, w_dec_all, emb_all, sems,
 ):
     for d in range(2):
         for q in range(4):
@@ -975,37 +976,52 @@
 
     E, EW, V, V8 = dims.E, dims.EW, dims.V, dims.V8
     steps = pl.num_programs(0)
+    V8, E8 = dims.V8, w_in_all.shape[1]
+    copies = [
+        pltpu.make_async_copy(w_in_all.at[:, 0:E], w_in_out, sems.at[0]),
+        pltpu.make_async_copy(w_dec_all.at[0:V], w_dec_out, sems.at[1]),
+        pltpu.make_async_copy(emb_all.at[0:V], emb_out, sems.at[2]),
+    ]
 
     @pl.when(pl.program_id(0) == 0)
     def _():
         for d in range(2):
             for q in range(4):
-                w_in_out[d, :, q, :] = gwin[d, q * EW : q * EW + E].astype(F32)
+                w_in_all[d, :, q, :] = gwin[d, q * EW : q * EW + EW].astype(F32)[0:E8]
                 first = q * EW + E // 16 * 16
                 row = gwin[d, first : first + 16].astype(F32)[E % 16 : E % 16 + 1]
                 b_in_out[d, q : q + 1, :] = row
                 b_rec_out[d, q : q + 1, :] = row
+        copies[0].start()
 
     @pl.when(pl.program_id(0) == steps // 4)
     def _():
         for d in range(2):
-            w_dec_out[:, d, :] = gwd[d, 0:V].astype(F32)
+            w_dec_all[:, d, :] = gwd[d].astype(F32)[0:V8]
+        copies[1].start()
 
     @pl.when(pl.program_id(0) == steps // 2)
     def _():
         for d in range(2):
-            emb_out[:, d, :] = small[d, 0:V, 0:E]
+            emb_all[:, d, :] = small[d, 0:V8, 0:E]
             for k in range(dims.VP // 128):
                 width = min(128, V - k * 128)
                 b_dec_out[d : d + 1, k * 128 : k * 128 + width] = small[d, V8 + k : V8 + k + 1, 0:width]
         at = V8 + dims.VP // 128
         loss_out[...] = small[0, at : at + 1, 0:1] + small[1, at : at + 1, 0:1]
+        copies[2].start()
+
+    @pl.when(pl.program_id(0) == steps - 1)
+    def _():
+        for copy in copies:
+            copy.wait()
 
 
 def call_outputs(dims, grec, gwin, gwd, small):
     KR, U2, E, V = dims.KR, dims.U2, dims.E, dims.V
     parts = 4 if KR % 64 == 0 else 1
     rows = KR // parts
+    apart = pl.BlockSpec(memory_space=pl.ANY)
 
     def whole(*shape):
         return pl.BlockSpec(shape, lambda i: (0,) * len(shape))
@@ -1019,7 +1035,14 @@
             pl.BlockSpec((2, 4, rows, U2), lambda i: (0, 0, i, 0)),
             whole(*gwin.shape), whole(*gwd.shape), whole(*small.shape),
         ],
-        out_specs=[pl.BlockSpec((2, rows, 4, U2), lambda i: (0, i, 0, 0))] + [whole(*s) for s in shapes],
+        out_specs=[pl.BlockSpec((2, rows, 4, U2), lambda i: (0, i, 0, 0))]
+        + [apart if len(s) > 2 and E in s or s[0] == V else whole(*s) for s in shapes],
+        scratch_shapes=[
+            pltpu.VMEM((2, ceil_to(E, 8), 4, U2), F32),
+            pltpu.VMEM((dims.V8, 2, U2), F32),
+            pltpu.VMEM((dims.V8, 2, E), F32),
+            pltpu.SemaphoreType.DMA((3,)),
+        ],
         compiler_params=pltpu.CompilerParams(vmem_limit_bytes=62 << 20),
         name="outputs",
     )(grec, gwin, gwd, small)

time: 238 us -> 238 us (level)
  no operation moved by 1% of the time
where the time goes in v7:
time: 238 us; the launch traced here: 237 us
  Pallas kernels  229 us (96%)
  local copies, waits for them, and re-layouts  7.16 us (3%)
    pallas_call x1, Pallas kernels, call_kernel(): pl.pallas_call(functools.partial(kernel, dims), out_shape=(jax.ShapeDtype...  222 us
    pallas_call x1, Pallas kernels, call_outputs(): pl.pallas_call(functools.partial(outputs_kernel, dims), grid=(parts,), ou...  6.33 us
    unnamed x8, local copies, waits for them, and re-layouts  5.13 us

profile of v7, /device:TPU:0, one launch (start us, length us, event | category | flops | bytes accessed | tf_op | source)
XLA Modules:
  0.0 237.5 jit_solution(3098763359998583501)
XLA Ops:
  0.6 0.0 copy-start.1
  0.6 1.0 copy.22
  1.6 0.7 fusion.2.emb_ref
  2.4 1.5 copy.23
  3.9 1.0 pad.14.clone
  4.8 0.0 copy-start
  4.8 0.0 copy-done.1
  4.8 0.2 copy.27
  5.0 1.1 pad.13.win_in
  6.1 0.7 copy-done
  6.8 1.7 copy.26
  8.5 222.4 %train_step.1 = (bf16[2,4,256,512]{3,2,1,0:T(8,128)(2,1)}, bf16[2,448,512]{2,1,0:T(8,128)(2,1)}, bf16[2,288,512]{2,1,0:T(8,128)(2,1)}, f32[2,288,128]{2,1,0:T(8,128)}) custom-call(s32[8,64]{1,0:T(8,128)} %bitcast.19, s32[2,8,64]{2,1,0:T(8,128)} %bitcast.18, s32[1,64]{1,0:T(1,128)} %bitcast.20, bf16[2,4,512]{2,1,0:T(4,128)(2,1)} %b_in_ref.1, ...), custom_call_target="tpu_custom_call" | custom-call | flops 30601641984 | bytes 8388608 | tf_op jit(solution)/shard_map/train_step/pallas_call | solution.py:950
  231.0 6.3 %outputs.1 = (f32[2,256,4,512]{3,2,1,0:T(4,128)}, f32[2,100,4,512]{3,2,1,0:T(4,128)}, f32[2,4,512]{2,1,0:T(4,128)}, f32[2,4,512]{2,1,0:T(4,128)}, f32[275,2,512]...) custom-call(bf16[2,4,256,512]{3,2,1,0:T(8,128)(2,1)} %get-tuple-element.20.grec, ...), custom_call_target="tpu_custom_call" | custom-call | tf_op jit(solution)/shard_map/outputs/pallas_call | solution.py:1030
Async XLA Ops:
  0.6 4.2 %copy-start.1 = (bf16[2,100,4,512]{3,2,1,0:T(4,128)(2,1)S(1)}, bf16[2,100,4,512]{3,2,1,0:T(4,128)(2,1)}, u32[]{:S(2)}) copy-start(bf16[2,100,4,512]{3,2,1,0:T(4,128)(2,1)} %param.16) | copy-start | bytes 2457604
  4.8 2.0 copy-start
